TPU v7x, 32 devices: a whole 2x2x4 slice. The times are simulated.
32 devices in a mesh: dp: 8 (over z, core), tensor: 4 (over y, x).
Axes of the slice: x: 2, y: 2, z: 4, core: 2. Of those that a mesh axis runs over, the one named last changes fastest.
Arguments:
- tokens: bfloat16 [6144, 1024], P('dp'), may hold values from -72 to 72
- w_qkv: float32 [1024, 3072], P(('dp', 'tensor')), may hold values from -0.1875 to 0.1875
- w_out: float32 [1024, 1024], P(None, ('dp', 'tensor')), may hold values from -0.1875 to 0.1875
- w_up: float32 [1024, 4096], P(('dp', 'tensor')), may hold values from -0.1875 to 0.1875
- w_down: float32 [4096, 1024], P(None, ('dp', 'tensor')), may hold values from -0.09375 to 0.09375
- slot_request: int32 [48, 128], replicated, may hold values from -1 to 3, as said below
Outputs:
- encoded: bfloat16 [6144, 1024], P('dp')
Inputs may be any that keep to these rules, and one draw needn't show every extreme that they name: `slot_request`: requests are numbered 0 to 3, all present; each request holds 1 to 24 pages and one holds exactly 24; each request's pages are full except its last page, whose empty slots are its final ones; pages may sit in any slot of the table.
All inputs are finite; a program needn't handle non-finite values.
Results may differ from a plain program's by a relative error of at most 0.025.
The roundings to bfloat16 on the way count: a program that leaves them out, or rounds other values in their place, can miss the bound.
Values may be sent and summed in bfloat16 or wider, within the bound.
A program may use at most 128 MiB of HBM per device.

v0:
```python
import math

import jax
import jax.numpy as jnp
from jax import lax
from jax.sharding import PartitionSpec as P

D = 1024
H = 16


def layer_norm(value):
    mean = jnp.mean(value, axis=-1, keepdims=True)
    centred = value - mean
    spread = jnp.mean(centred * centred, axis=-1, keepdims=True)
    return centred * lax.rsqrt(spread + 1e-05)


def shards(tokens, w_qkv, w_out, w_up, w_down, slot_request):
    groups = lax.axis_size("tensor")
    tensor_rank = lax.axis_index("tensor")
    row_split = (w_qkv.astype(jnp.bfloat16), w_up.astype(jnp.bfloat16))
    col_split = (w_out.astype(jnp.bfloat16), w_down.astype(jnp.bfloat16))
    qkv_full, up_full = (
        lax.all_gather(row_split[0], ("dp", "tensor"), axis=0, tiled=True),
        lax.all_gather(row_split[1], ("dp", "tensor"), axis=0, tiled=True),
    )
    out_full, down_full = (
        lax.all_gather(col_split[0], ("dp", "tensor"), axis=1, tiled=True),
        lax.all_gather(col_split[1], ("dp", "tensor"), axis=1, tiled=True),
    )
    qkv_cols = qkv_full.shape[1] // groups
    up_cols = up_full.shape[1] // groups
    out_rows = out_full.shape[0] // groups
    down_rows = down_full.shape[0] // groups
    qkv_block = lax.dynamic_slice_in_dim(qkv_full, tensor_rank * qkv_cols, qkv_cols, 1)
    up_block = lax.dynamic_slice_in_dim(up_full, tensor_rank * up_cols, up_cols, 1)
    out_block = lax.dynamic_slice_in_dim(out_full, tensor_rank * out_rows, out_rows, 0)
    down_block = lax.dynamic_slice_in_dim(down_full, tensor_rank * down_rows, down_rows, 0)
    tok_rows = tokens.shape[0]
    head_size = D // H
    heads_here = qkv_block.shape[1] // (3 * head_size)
    qkv = jnp.dot(tokens, qkv_block, preferred_element_type=jnp.float32).astype(jnp.bfloat16)
    qkv = qkv.reshape(tok_rows, heads_here, 3, head_size)
    queries = qkv[:, :, 0, :]
    key_rows = qkv[:, :, 1, :].reshape(tok_rows, heads_here * head_size)
    value_rows = qkv[:, :, 2, :].reshape(tok_rows, heads_here * head_size)
    slot_ids = slot_request.reshape(-1)
    own_ids = lax.dynamic_slice_in_dim(slot_ids, lax.axis_index("dp") * tok_rows, tok_rows, 0)
    scale = 1.0 / math.sqrt(head_size)

    def update(carry, key_block, value_block, key_ids):
        running_max, total, accumulated = carry
        width = key_block.shape[0]
        key_heads = key_block.reshape(width, heads_here, head_size)
        value_heads = value_block.reshape(width, heads_here, head_size)
        scores = (
            jnp.einsum("qhd,khd->hqk", queries, key_heads, preferred_element_type=jnp.float32)
            * scale
        )
        allowed = (own_ids[:, None] == key_ids[None, :])[None]
        masked = jnp.where(allowed, scores, -1e30)
        new_max = jnp.maximum(running_max, jnp.max(masked, axis=-1))
        weights = jnp.where(allowed, jnp.exp(masked - new_max[..., None]), 0.0)
        rescale = jnp.exp(running_max - new_max)
        total = total * rescale + jnp.sum(weights, axis=-1)
        mixed = jnp.einsum(
            "hqk,khd->qhd",
            weights.astype(jnp.bfloat16),
            value_heads,
            preferred_element_type=jnp.float32,
        )
        accumulated = accumulated * jnp.transpose(rescale)[..., None] + mixed
        return (new_max, total, accumulated)

    def visit(carry, key_block, value_block, key_ids):
        return update(carry, key_block, value_block, key_ids)

    initial = (
        jnp.full((heads_here, tok_rows), -1e30, jnp.float32),
        jnp.zeros((heads_here, tok_rows), jnp.float32),
        jnp.zeros((tok_rows, heads_here, head_size), jnp.float32),
    )
    key_piece = lax.all_gather(key_rows, "dp", axis=0, tiled=True)
    value_piece = lax.all_gather(value_rows, "dp", axis=0, tiled=True)
    key_count = key_piece.shape[0]
    steps = key_count // tok_rows
    piece_ids = slot_ids.reshape(steps, tok_rows)
    key_steps = key_piece.reshape(steps, tok_rows, key_piece.shape[1])
    value_steps = value_piece.reshape(steps, tok_rows, value_piece.shape[1])

    def one_step(state, inputs):
        key_block, value_block, key_ids = inputs
        return (visit(state, key_block, value_block, key_ids), None)

    result, unused = lax.scan(one_step, initial, (key_steps, value_steps, piece_ids))
    running_max, total, accumulated = result
    attn = (
        (accumulated / jnp.transpose(total)[..., None])
        .astype(jnp.bfloat16)
        .reshape(tok_rows, heads_here * head_size)
    )
    proj = lax.psum(
        jnp.dot(attn, out_block, preferred_element_type=jnp.float32).astype(jnp.bfloat16), "tensor"
    ).astype(jnp.float32)
    first = layer_norm(tokens.astype(jnp.float32) + proj).astype(jnp.bfloat16)
    inner = jax.nn.gelu(
        jnp.dot(first, up_block, preferred_element_type=jnp.float32), approximate=False
    ).astype(jnp.bfloat16)
    ffn = lax.psum(
        jnp.dot(inner, down_block, preferred_element_type=jnp.float32).astype(jnp.bfloat16),
        "tensor",
    ).astype(jnp.float32)
    live = (own_ids >= 0).astype(jnp.float32)[:, None]
    encoded = (layer_norm(first.astype(jnp.float32) + ffn) * live).astype(jnp.bfloat16)
    return encoded


def solution(mesh):
    in_specs = (
        P("dp", None),
        P(("dp", "tensor"), None),
        P(None, ("dp", "tensor")),
        P(("dp", "tensor"), None),
        P(None, ("dp", "tensor")),
        P(),
    )
    out_specs = P("dp", None)
    return jax.shard_map(shards, mesh=mesh, in_specs=in_specs, out_specs=out_specs, check_vma=False)
```

profile of v0, /device:TPU:0, one launch (start us, length us, event | category | flops | bytes accessed | tf_op | source)
XLA Modules:
  0.0 614.2 jit_solution(3064696481038361507)
XLA Ops:
  6.5 1.7 convert_element_type.55
  8.3 74.3 %all-gather.7.cloned.1.call-done = bf16[1024,3072]{1,0:T(8,128)(2,1)} async-done(((bf16[32,3072]{1,0:T(8,128)(2,1)}), bf16[1024,3072]{1,0:T(8,128)(2,1)}) %all-gather.7.cloned.1.call-update) | async-done | bytes 6291472 | tf_op jit(solution)/shard_map/all_gather | solution.py:25
  82.6 3.3 fusion.70
  85.9 1.0 fusion.112
  87.0 0.7 all-gather.11.cloned.1.call-update
  87.7 0.6 convert_element_type.59
  88.6 35.3 %all-gather.9.cloned.1.call-done = bf16[6144,256]{0,1:T(8,128)(2,1)} async-done(((bf16[768,256]{0,1:T(8,128)(2,1)}), bf16[6144,256]{0,1:T(8,128)(2,1)}) %all-gather.9.cloned.1.call-update) | async-done | bytes 3145744 | tf_op jit(solution)/shard_map/all_gather | solution.py:84
  123.9 4.7 copy.17
  128.6 34.1 %all-gather.11.cloned.1.call-done = bf16[6144,256]{0,1:T(8,128)(2,1)} async-done(((bf16[768,256]{0,1:T(8,128)(2,1)}), bf16[6144,256]{0,1:T(8,128)(2,1)}) %all-gather.11.cloned.1.call-update) | async-done | bytes 3145744 | tf_op jit(solution)/shard_map/all_gather | solution.py:85
  162.7 4.7 copy.20
  167.4 138.5 %while.15 = (s32[]{:T(128)}, f32[4,768]{1,0:T(4,128)S(1)}, f32[4,768]{1,0:T(4,128)S(1)}, f32[768,4,64]{0,2,1:T(8,128)}, s32[768]{0:T(1024)S(1)}, /*index=5*/s32[...) while((s32[]{:T(128)}, f32[4,768]{1,0:T(4,128)S(1)}, ...), condition=%wide.region_3.4_spmd.clone, body=%wide.region_0.3_spmd.clone.sunk | while | flops 635848704 | bytes 65089736 | solution.py:96
  167.4 0.4 broadcast_compare_fusion.2
  167.9 1.2 constant_dynamic-slice_fusion.3
  169.2 5.4 fusion.132
  174.8 7.4 %fusion.136 = f32[768,4,64]{0,2,1:T(8,128)} fusion(bf16[768,4,64]{0,2,1:T(8,128)(2,1)S(1)} %bitcast.70, f32[4,768,768]{2,1,0:T(8,128)} %get-tuple-element.196, f32[4,768]{1,0:T(4,128)S(1)} %get-tuple-element.222, pred[768,768]{0,1:T(8,128)(4,1)S(1)} %broadcast_compare_fusion.2, f32[768,4,64]{0,2,1:T(8,128)} %get-tuple-element.213, ...), kind=kOutput, calls=%fused_computation.8.clone.1 | convolution fusion | flops 314376192 | bytes 12017665 | tf_op jit(solution)/shard_map/while/body/eval_jaxpr/hqk,khd->qhd/dot_general | solution.py:67
  182.2 2.3 fusion.134
  184.6 0.4 broadcast_compare_fusion.2
  185.0 1.2 constant_dynamic-slice_fusion.3
  186.4 5.4 fusion.132
  192.0 7.5 %fusion.136 = f32[768,4,64]{0,2,1:T(8,128)} fusion(bf16[768,4,64]{0,2,1:T(8,128)(2,1)S(1)} %bitcast.70, f32[4,768,768]{2,1,0:T(8,128)} %get-tuple-element.196, f32[4,768]{1,0:T(4,128)S(1)} %get-tuple-element.222, pred[768,768]{0,1:T(8,128)(4,1)S(1)} %broadcast_compare_fusion.2, f32[768,4,64]{0,2,1:T(8,128)} %get-tuple-element.213, ...), kind=kOutput, calls=%fused_computation.8.clone.1 | convolution fusion | flops 314376192 | bytes 12017665 | tf_op jit(solution)/shard_map/while/body/eval_jaxpr/hqk,khd->qhd/dot_general | solution.py:67
  199.6 2.3 fusion.134
  202.0 0.4 broadcast_compare_fusion.2
  202.4 1.2 constant_dynamic-slice_fusion.3
  203.7 5.4 fusion.132
  209.4 7.6 %fusion.136 = f32[768,4,64]{0,2,1:T(8,128)} fusion(bf16[768,4,64]{0,2,1:T(8,128)(2,1)S(1)} %bitcast.70, f32[4,768,768]{2,1,0:T(8,128)} %get-tuple-element.196, f32[4,768]{1,0:T(4,128)S(1)} %get-tuple-element.222, pred[768,768]{0,1:T(8,128)(4,1)S(1)} %broadcast_compare_fusion.2, f32[768,4,64]{0,2,1:T(8,128)} %get-tuple-element.213, ...), kind=kOutput, calls=%fused_computation.8.clone.1 | convolution fusion | flops 314376192 | bytes 12017665 | tf_op jit(solution)/shard_map/while/body/eval_jaxpr/hqk,khd->qhd/dot_general | solution.py:67
  217.0 2.3 fusion.134
  219.4 0.4 broadcast_compare_fusion.2
  219.8 1.2 constant_dynamic-slice_fusion.3
  221.1 5.4 fusion.132
  226.7 7.5 %fusion.136 = f32[768,4,64]{0,2,1:T(8,128)} fusion(bf16[768,4,64]{0,2,1:T(8,128)(2,1)S(1)} %bitcast.70, f32[4,768,768]{2,1,0:T(8,128)} %get-tuple-element.196, f32[4,768]{1,0:T(4,128)S(1)} %get-tuple-element.222, pred[768,768]{0,1:T(8,128)(4,1)S(1)} %broadcast_compare_fusion.2, f32[768,4,64]{0,2,1:T(8,128)} %get-tuple-element.213, ...), kind=kOutput, calls=%fused_computation.8.clone.1 | convolution fusion | flops 314376192 | bytes 12017665 | tf_op jit(solution)/shard_map/while/body/eval_jaxpr/hqk,khd->qhd/dot_general | solution.py:67
  234.3 2.3 fusion.134
  237.1 1.2 constant_dynamic-slice_fusion.3
  238.4 5.4 fusion.132
  244.1 7.5 %fusion.136 = f32[768,4,64]{0,2,1:T(8,128)} fusion(bf16[768,4,64]{0,2,1:T(8,128)(2,1)S(1)} %bitcast.70, f32[4,768,768]{2,1,0:T(8,128)} %get-tuple-element.196, f32[4,768]{1,0:T(4,128)S(1)} %get-tuple-element.222, pred[768,768]{0,1:T(8,128)(4,1)S(1)} %broadcast_compare_fusion.2, f32[768,4,64]{0,2,1:T(8,128)} %get-tuple-element.213, ...), kind=kOutput, calls=%fused_computation.8.clone.1 | convolution fusion | flops 314376192 | bytes 12017665 | tf_op jit(solution)/shard_map/while/body/eval_jaxpr/hqk,khd->qhd/dot_general | solution.py:67
  251.6 2.3 fusion.134
  254.4 1.2 constant_dynamic-slice_fusion.3
  255.8 5.4 fusion.132
  261.4 7.5 %fusion.136 = f32[768,4,64]{0,2,1:T(8,128)} fusion(bf16[768,4,64]{0,2,1:T(8,128)(2,1)S(1)} %bitcast.70, f32[4,768,768]{2,1,0:T(8,128)} %get-tuple-element.196, f32[4,768]{1,0:T(4,128)S(1)} %get-tuple-element.222, pred[768,768]{0,1:T(8,128)(4,1)S(1)} %broadcast_compare_fusion.2, f32[768,4,64]{0,2,1:T(8,128)} %get-tuple-element.213, ...), kind=kOutput, calls=%fused_computation.8.clone.1 | convolution fusion | flops 314376192 | bytes 12017665 | tf_op jit(solution)/shard_map/while/body/eval_jaxpr/hqk,khd->qhd/dot_general | solution.py:67
  268.9 2.3 fusion.134
  271.3 0.4 broadcast_compare_fusion.2
  271.7 1.2 constant_dynamic-slice_fusion.3
  273.1 5.4 fusion.132
  278.7 7.5 %fusion.136 = f32[768,4,64]{0,2,1:T(8,128)} fusion(bf16[768,4,64]{0,2,1:T(8,128)(2,1)S(1)} %bitcast.70, f32[4,768,768]{2,1,0:T(8,128)} %get-tuple-element.196, f32[4,768]{1,0:T(4,128)S(1)} %get-tuple-element.222, pred[768,768]{0,1:T(8,128)(4,1)S(1)} %broadcast_compare_fusion.2, f32[768,4,64]{0,2,1:T(8,128)} %get-tuple-element.213, ...), kind=kOutput, calls=%fused_computation.8.clone.1 | convolution fusion | flops 314376192 | bytes 12017665 | tf_op jit(solution)/shard_map/while/body/eval_jaxpr/hqk,khd->qhd/dot_general | solution.py:67
  286.3 2.3 fusion.134
  288.6 0.4 broadcast_compare_fusion.2
  289.0 1.2 constant_dynamic-slice_fusion.3
  290.4 5.4 fusion.132
  296.0 7.5 %fusion.136 = f32[768,4,64]{0,2,1:T(8,128)} fusion(bf16[768,4,64]{0,2,1:T(8,128)(2,1)S(1)} %bitcast.70, f32[4,768,768]{2,1,0:T(8,128)} %get-tuple-element.196, f32[4,768]{1,0:T(4,128)S(1)} %get-tuple-element.222, pred[768,768]{0,1:T(8,128)(4,1)S(1)} %broadcast_compare_fusion.2, f32[768,4,64]{0,2,1:T(8,128)} %get-tuple-element.213, ...), kind=kOutput, calls=%fused_computation.8.clone.1 | convolution fusion | flops 314376192 | bytes 12017665 | tf_op jit(solution)/shard_map/while/body/eval_jaxpr/hqk,khd->qhd/dot_general | solution.py:67
  303.6 2.3 fusion.134
  306.0 1.3 divide_convert_fusion
  307.3 2.9 convolution_convert_fusion
  310.3 0.7 convert_element_type.64
  311.1 0.8 convert_element_type.66
  312.1 58.0 %all-reduce.3.cloned.1.call-done = bf16[768,1024]{1,0:T(8,128)(2,1)} async-done(((bf16[768,1024]{1,0:T(8,128)(2,1)}), bf16[768,1024]{1,0:T(8,128)(2,1)}) %all-reduce.3.cloned.1.call-update) | async-done | bytes 1572880 | tf_op jit(solution)/shard_map/psum | solution.py:103
  370.1 2.0 fusion.28
  372.2 0.7 multiply_reduce_fusion.1
  372.9 0.6 multiply_convert_fusion.1
  373.5 77.4 %all-gather.15.cloned.1.call-done = bf16[1024,4096]{1,0:T(8,128)(2,1)} async-done(((bf16[32,4096]{1,0:T(8,128)(2,1)}), bf16[1024,4096]{1,0:T(8,128)(2,1)}) %all-gather.15.cloned.1.call-update) | async-done | bytes 8388624 | tf_op jit(solution)/shard_map/all_gather | solution.py:26
  450.9 79.5 %all-gather.17.cloned.1.call-done = bf16[4096,1024]{0,1:T(8,128)(2,1)} async-done(((bf16[4096,32]{0,1:T(8,128)(2,1)}), bf16[4096,1024]{0,1:T(8,128)(2,1)}) %all-gather.17.cloned.1.call-update) | async-done | bytes 8388624 | tf_op jit(solution)/shard_map/all_gather | solution.py:30
  530.3 12.7 %fusion.35 = bf16[768,1024]{1,0:T(8,128)(2,1)} fusion(bf16[4096,1024]{0,1:T(8,128)(2,1)} %all-gather.17.cloned.1.call-done, s32[]{:T(128)S(6)} %select_n.23, bf16[768,1024]{1,0:T(8,128)(2,1)S(1)} %multiply_convert_fusion.1, bf16[1024,4096]{1,0:T(8,128)(2,1)} %all-gather.15.cloned.1.call-done), kind=kOutput, calls=%fused_computation.55 | convolution fusion | flops 3273129984 | bytes 7341056 | tf_op jit(solution)/shard_map/dot_general | solution.py:111
  543.0 59.7 %all-reduce.5.cloned.1.call-done = bf16[768,1024]{1,0:T(8,128)(2,1)} async-done(((bf16[768,1024]{1,0:T(8,128)(2,1)}), bf16[768,1024]{1,0:T(8,128)(2,1)}) %all-reduce.5.cloned.1.call-update) | async-done | bytes 1572880 | tf_op jit(solution)/shard_map/psum | solution.py:110
  602.7 2.0 fusion.30
  604.7 0.7 multiply_reduce_fusion
  605.4 1.9 multiply_convert_fusion
  (145 shorter events, 4.9 us)
Async XLA Ops:
  6.5 76.0 %all-gather.7.cloned.1.call-start = ((), (), s32[]{:S(2)}) async-start(), calls=%async_computation | async-start | bytes 6488064 | tf_op jit(solution)/shard_map/all_gather | solution.py:25
  8.3 115.7 %all-gather.9.cloned.1.call-start = ((), (), s32[]{:S(2)}) async-start(), calls=%async_computation.1 | async-start | bytes 3538944 | tf_op jit(solution)/shard_map/all_gather | solution.py:84
  85.9 1.8 copy-start.5
  85.9 2.6 copy-start.6
  86.9 75.8 %all-gather.11.cloned.1.call-start = ((), (), s32[]{:S(2)}) async-start(), calls=%async_computation.2 | async-start | bytes 3538944 | tf_op jit(solution)/shard_map/all_gather | solution.py:85
  87.7 219.6 %all-gather.13.cloned.1.call-start = ((), (), s32[]{:S(2)}) async-start(), calls=%async_computation.3 | async-start | bytes 2162688 | tf_op jit(solution)/shard_map/all_gather | solution.py:29
  88.4 281.7 %all-reduce.3.cloned.1.call-start = ((), (), s32[]{:S(2)}) async-start(), calls=%async_computation.4 | async-start | bytes 3145728 | tf_op jit(solution)/shard_map/psum | solution.py:103
  174.6 7.6 %slice-start = ((s8[9437184]{0:T(1024)(128)(4,1)}), s8[1048576]{0:T(1024)(128)(4,1)S(1)}, s32[]{:S(2)}) async-start(s8[9437184]{0:T(1024)(128)(4,1)} %bitcast.67), calls=%async_computation.8 | async-start | bytes 2097152 | tf_op jit(solution)/shard_map/while
  174.8 7.4 %slice-start.1 = ((s8[9437184]{0:T(1024)(128)(4,1)}), s8[4194304]{0:T(1024)(128)(4,1)S(1)}, s32[]{:S(2)}) async-start(s8[9437184]{0:T(1024)(128)(4,1)} %bitcast.67), calls=%async_computation.9 | async-start | bytes 8388608 | tf_op jit(solution)/shard_map/while
  174.8 7.4 %slice-start.2 = ((s8[9437184]{0:T(1024)(128)(4,1)}), s8[4194304]{0:T(1024)(128)(4,1)S(1)}, s32[]{:S(2)}) async-start(s8[9437184]{0:T(1024)(128)(4,1)} %bitcast.67), calls=%async_computation.10 | async-start | bytes 8388608 | tf_op jit(solution)/shard_map/while
  191.8 7.8 %slice-start = ((s8[9437184]{0:T(1024)(128)(4,1)}), s8[1048576]{0:T(1024)(128)(4,1)S(1)}, s32[]{:S(2)}) async-start(s8[9437184]{0:T(1024)(128)(4,1)} %bitcast.67), calls=%async_computation.8 | async-start | bytes 2097152 | tf_op jit(solution)/shard_map/while
  192.0 7.6 %slice-start.1 = ((s8[9437184]{0:T(1024)(128)(4,1)}), s8[4194304]{0:T(1024)(128)(4,1)S(1)}, s32[]{:S(2)}) async-start(s8[9437184]{0:T(1024)(128)(4,1)} %bitcast.67), calls=%async_computation.9 | async-start | bytes 8388608 | tf_op jit(solution)/shard_map/while
  192.0 7.6 %slice-start.2 = ((s8[9437184]{0:T(1024)(128)(4,1)}), s8[4194304]{0:T(1024)(128)(4,1)S(1)}, s32[]{:S(2)}) async-start(s8[9437184]{0:T(1024)(128)(4,1)} %bitcast.67), calls=%async_computation.10 | async-start | bytes 8388608 | tf_op jit(solution)/shard_map/while
  209.2 7.8 %slice-start = ((s8[9437184]{0:T(1024)(128)(4,1)}), s8[1048576]{0:T(1024)(128)(4,1)S(1)}, s32[]{:S(2)}) async-start(s8[9437184]{0:T(1024)(128)(4,1)} %bitcast.67), calls=%async_computation.8 | async-start | bytes 2097152 | tf_op jit(solution)/shard_map/while
  209.3 7.6 %slice-start.1 = ((s8[9437184]{0:T(1024)(128)(4,1)}), s8[4194304]{0:T(1024)(128)(4,1)S(1)}, s32[]{:S(2)}) async-start(s8[9437184]{0:T(1024)(128)(4,1)} %bitcast.67), calls=%async_computation.9 | async-start | bytes 8388608 | tf_op jit(solution)/shard_map/while
  209.3 7.6 %slice-start.2 = ((s8[9437184]{0:T(1024)(128)(4,1)}), s8[4194304]{0:T(1024)(128)(4,1)S(1)}, s32[]{:S(2)}) async-start(s8[9437184]{0:T(1024)(128)(4,1)} %bitcast.67), calls=%async_computation.10 | async-start | bytes 8388608 | tf_op jit(solution)/shard_map/while
  226.5 7.7 %slice-start = ((s8[9437184]{0:T(1024)(128)(4,1)}), s8[1048576]{0:T(1024)(128)(4,1)S(1)}, s32[]{:S(2)}) async-start(s8[9437184]{0:T(1024)(128)(4,1)} %bitcast.67), calls=%async_computation.8 | async-start | bytes 2097152 | tf_op jit(solution)/shard_map/while
  226.7 7.6 %slice-start.1 = ((s8[9437184]{0:T(1024)(128)(4,1)}), s8[4194304]{0:T(1024)(128)(4,1)S(1)}, s32[]{:S(2)}) async-start(s8[9437184]{0:T(1024)(128)(4,1)} %bitcast.67), calls=%async_computation.9 | async-start | bytes 8388608 | tf_op jit(solution)/shard_map/while
  226.7 7.5 %slice-start.2 = ((s8[9437184]{0:T(1024)(128)(4,1)}), s8[4194304]{0:T(1024)(128)(4,1)S(1)}, s32[]{:S(2)}) async-start(s8[9437184]{0:T(1024)(128)(4,1)} %bitcast.67), calls=%async_computation.10 | async-start | bytes 8388608 | tf_op jit(solution)/shard_map/while
  243.8 7.7 %slice-start = ((s8[9437184]{0:T(1024)(128)(4,1)}), s8[1048576]{0:T(1024)(128)(4,1)S(1)}, s32[]{:S(2)}) async-start(s8[9437184]{0:T(1024)(128)(4,1)} %bitcast.67), calls=%async_computation.8 | async-start | bytes 2097152 | tf_op jit(solution)/shard_map/while
  244.0 7.6 %slice-start.1 = ((s8[9437184]{0:T(1024)(128)(4,1)}), s8[4194304]{0:T(1024)(128)(4,1)S(1)}, s32[]{:S(2)}) async-start(s8[9437184]{0:T(1024)(128)(4,1)} %bitcast.67), calls=%async_computation.9 | async-start | bytes 8388608 | tf_op jit(solution)/shard_map/while
  244.0 7.5 %slice-start.2 = ((s8[9437184]{0:T(1024)(128)(4,1)}), s8[4194304]{0:T(1024)(128)(4,1)S(1)}, s32[]{:S(2)}) async-start(s8[9437184]{0:T(1024)(128)(4,1)} %bitcast.67), calls=%async_computation.10 | async-start | bytes 8388608 | tf_op jit(solution)/shard_map/while
  261.2 7.7 %slice-start = ((s8[9437184]{0:T(1024)(128)(4,1)}), s8[1048576]{0:T(1024)(128)(4,1)S(1)}, s32[]{:S(2)}) async-start(s8[9437184]{0:T(1024)(128)(4,1)} %bitcast.67), calls=%async_computation.8 | async-start | bytes 2097152 | tf_op jit(solution)/shard_map/while
  261.4 7.6 %slice-start.1 = ((s8[9437184]{0:T(1024)(128)(4,1)}), s8[4194304]{0:T(1024)(128)(4,1)S(1)}, s32[]{:S(2)}) async-start(s8[9437184]{0:T(1024)(128)(4,1)} %bitcast.67), calls=%async_computation.9 | async-start | bytes 8388608 | tf_op jit(solution)/shard_map/while
  261.4 7.5 %slice-start.2 = ((s8[9437184]{0:T(1024)(128)(4,1)}), s8[4194304]{0:T(1024)(128)(4,1)S(1)}, s32[]{:S(2)}) async-start(s8[9437184]{0:T(1024)(128)(4,1)} %bitcast.67), calls=%async_computation.10 | async-start | bytes 8388608 | tf_op jit(solution)/shard_map/while
  278.5 7.7 %slice-start = ((s8[9437184]{0:T(1024)(128)(4,1)}), s8[1048576]{0:T(1024)(128)(4,1)S(1)}, s32[]{:S(2)}) async-start(s8[9437184]{0:T(1024)(128)(4,1)} %bitcast.67), calls=%async_computation.8 | async-start | bytes 2097152 | tf_op jit(solution)/shard_map/while
  278.7 7.6 %slice-start.1 = ((s8[9437184]{0:T(1024)(128)(4,1)}), s8[4194304]{0:T(1024)(128)(4,1)S(1)}, s32[]{:S(2)}) async-start(s8[9437184]{0:T(1024)(128)(4,1)} %bitcast.67), calls=%async_computation.9 | async-start | bytes 8388608 | tf_op jit(solution)/shard_map/while
  278.7 7.5 %slice-start.2 = ((s8[9437184]{0:T(1024)(128)(4,1)}), s8[4194304]{0:T(1024)(128)(4,1)S(1)}, s32[]{:S(2)}) async-start(s8[9437184]{0:T(1024)(128)(4,1)} %bitcast.67), calls=%async_computation.10 | async-start | bytes 8388608 | tf_op jit(solution)/shard_map/while
  295.8 7.7 %slice-start = ((s8[9437184]{0:T(1024)(128)(4,1)}), s8[1048576]{0:T(1024)(128)(4,1)S(1)}, s32[]{:S(2)}) async-start(s8[9437184]{0:T(1024)(128)(4,1)} %bitcast.67), calls=%async_computation.8 | async-start | bytes 2097152 | tf_op jit(solution)/shard_map/while
  296.0 7.6 %slice-start.1 = ((s8[9437184]{0:T(1024)(128)(4,1)}), s8[4194304]{0:T(1024)(128)(4,1)S(1)}, s32[]{:S(2)}) async-start(s8[9437184]{0:T(1024)(128)(4,1)} %bitcast.67), calls=%async_computation.9 | async-start | bytes 8388608 | tf_op jit(solution)/shard_map/while
  296.0 7.5 %slice-start.2 = ((s8[9437184]{0:T(1024)(128)(4,1)}), s8[4194304]{0:T(1024)(128)(4,1)S(1)}, s32[]{:S(2)}) async-start(s8[9437184]{0:T(1024)(128)(4,1)} %bitcast.67), calls=%async_computation.10 | async-start | bytes 8388608 | tf_op jit(solution)/shard_map/while
  305.9 4.3 copy-start.3
  305.9 5.2 copy-start.4
  307.2 62.9 %copy-start = (bf16[768,1024]{1,0:T(8,128)(2,1)S(1)}, bf16[768,1024]{1,0:T(8,128)(2,1)}, u32[]{:S(2)}) copy-start(bf16[768,1024]{1,0:T(8,128)(2,1)} %param.8) | copy-start | bytes 4718596
  310.2 140.6 %all-gather.15.cloned.1.call-start = ((), (), s32[]{:S(2)}) async-start(), calls=%async_computation.5 | async-start | bytes 8650752 | tf_op jit(solution)/shard_map/all_gather | solution.py:26
  311.1 219.3 %all-gather.17.cloned.1.call-start = ((), (), s32[]{:S(2)}) async-start(), calls=%async_computation.6 | async-start | bytes 8650752 | tf_op jit(solution)/shard_map/all_gather | solution.py:30
  311.9 290.8 %all-reduce.5.cloned.1.call-start = ((), (), s32[]{:S(2)}) async-start(), calls=%async_computation.7 | async-start | bytes 3145728 | tf_op jit(solution)/shard_map/psum | solution.py:110
  370.1 2.0 copy-start.1
  602.7 2.0 copy-start.2
Sparse Core Ops, SparseCore 0:
  10.2 72.2 all-gather.6
  87.0 36.8 all-gather.8
  125.5 37.1 all-gather.10
  165.4 55.3 all-gather.12
  310.4 59.7 all-reduce.2
  373.3 77.5 all-gather.14
  454.1 76.1 all-gather.16
  543.1 59.4 all-reduce.4
where the time goes:
time: 615 us; the launch traced here: 614 us
  waiting for transfers between devices  419 us (68%)
  matrix products  122 us (20%)
  other arithmetic  35.1 us (6%)
  local copies, waits for them, and re-layouts  22.8 us (4%)
  between operations  13.7 us (2%)
    all_gather x1, waiting for transfers between devices, shards(): lax.all_gather(col_split[1], ('dp', 'tensor'), axis=1, tiled=True)  79.5 us
    all_gather x1, waiting for transfers between devices, shards(): lax.all_gather(row_split[1], ('dp', 'tensor'), axis=0, tiled=True)  77.4 us
    all_gather x1, waiting for transfers between devices, shards(): lax.all_gather(row_split[0], ('dp', 'tensor'), axis=0, tiled=True)  74.3 us
    dot_general x8, matrix products, update(): jnp.einsum('hqk,khd->qhd', weights.astype(jnp.bfloat16), value_heads, pre...  60.2 us
    psum x1, waiting for transfers between devices, shards(): lax.psum(jnp.dot(inner, down_block, preferred_element_type=jnp.float32).a...  59.7 us
    psum x1, waiting for transfers between devices, shards(): lax.psum(jnp.dot(attn, out_block, preferred_element_type=jnp.float32).ast...  58 us
    dot_general x8, matrix products, update(): jnp.einsum('qhd,khd->hqk', queries, key_heads, preferred_element_type=jnp...  43.2 us
    all_gather x1, waiting for transfers between devices, shards(): key_piece = lax.all_gather(key_rows, 'dp', axis=0, tiled=True)  35.3 us
  transfers between devices with their start and end apart: 8, of which 7 were waited for; matrix products, arithmetic and copies ran while one was open for 25% of the time, Pallas kernels for 0%

commit v1 on v0

v1 whole, which is shorter than its diff:
```python
import functools

import jax
import jax.numpy as jnp
from jax import lax
from jax.experimental import pallas as pl
from jax.experimental.pallas import tpu as pltpu
from jax.sharding import PartitionSpec as P

HEAD = 64
MESH = pl.DeviceIdType.MESH
GROUP = 4
BF = jnp.bfloat16
F32 = jnp.float32


def greet(targets):
    barrier = pltpu.get_barrier_semaphore()
    for cond, dev in targets:
        if cond is None:
            pl.semaphore_signal(barrier, inc=1, device_id=dev, device_id_type=MESH)
        else:

            @pl.when(cond)
            def _(dev=dev):
                pl.semaphore_signal(barrier, inc=1, device_id=dev, device_id_type=MESH)

    count = sum(1 if cond is None else jnp.where(cond, 1, 0) for cond, _ in targets)
    pl.semaphore_wait(barrier, count)


def exchange_kernel(groups, x_ref, out_ref, send_sem, recv_sem, local_sem):
    dp = lax.axis_index("dp")
    me = lax.axis_index("tensor")
    greet([(None, (dp, lax.rem(me + k, groups))) for k in range(1, groups)])
    local = pltpu.make_async_copy(x_ref.at[me], out_ref.at[me], local_sem)
    local.start()
    sends = []
    for k in range(1, groups):
        peer = lax.rem(me + k, groups)
        copy = pltpu.make_async_remote_copy(
            x_ref.at[peer], out_ref.at[me], send_sem.at[k], recv_sem.at[k],
            device_id=(dp, peer), device_id_type=MESH,
        )
        copy.start()
        sends.append(copy)
    for copy in sends:
        copy.wait()
    local.wait()


def exchange(x, groups, cid):
    return pl.pallas_call(
        functools.partial(exchange_kernel, groups),
        out_shape=jax.ShapeDtypeStruct(x.shape, x.dtype),
        in_specs=[pl.BlockSpec(memory_space=pl.ANY)],
        out_specs=pl.BlockSpec(memory_space=pl.ANY),
        scratch_shapes=[
            pltpu.SemaphoreType.DMA((groups,)),
            pltpu.SemaphoreType.DMA((groups,)),
            pltpu.SemaphoreType.DMA,
        ],
        compiler_params=pltpu.CompilerParams(collective_id=cid, has_side_effects=True),
        name="exchange",
    )(x)


def gather_kernel(chips, x_ref, out_ref, right_sem, left_sem, core_sem, recv_sem, local_sem):
    dp = lax.axis_index("dp")
    tensor = lax.axis_index("tensor")
    chip, core = dp // 2, lax.rem(dp, 2)
    other = 1 - core
    partner = (2 * chip + other, tensor)
    has_right, has_left = chip + 1 < chips, chip > 0
    right = (2 * jnp.minimum(chip + 1, chips - 1) + core, tensor)
    left = (2 * jnp.maximum(chip - 1, 0) + core, tensor)
    greet([(None, partner), (has_right, right), (has_left, left)])
    local = pltpu.make_async_copy(x_ref, out_ref.at[dp], local_sem)
    local.start()

    def copy_of(source, block, send, device):
        return pltpu.make_async_remote_copy(
            source, out_ref.at[block], send, recv_sem.at[block],
            device_id=device, device_id_type=MESH,
        )

    @pl.when(has_right)
    def _():
        copy_of(x_ref, dp, right_sem.at[0], right).start()

    @pl.when(has_left)
    def _():
        copy_of(x_ref, dp, left_sem.at[0], left).start()

    copy_of(x_ref, dp, core_sem.at[chip], partner).start()
    for s in range(1, chips):
        for away, has_next, sems, following in (
            (chip - s, has_right, right_sem, right),
            (chip + s, has_left, left_sem, left),
        ):

            @pl.when(jnp.logical_and(away >= 0, away < chips))
            def _(away=away, has_next=has_next, sems=sems, following=following, s=s):
                block = 2 * away + core
                copy_of(out_ref.at[block], block, core_sem.at[away], partner).wait_recv()

                @pl.when(has_next)
                def _():
                    copy_of(out_ref.at[block], block, sems.at[s], following).start()

                copy_of(out_ref.at[block], block, core_sem.at[away], partner).start()

    for away in range(chips):
        block = 2 * away + other
        copy_of(x_ref, block, core_sem.at[away], partner).wait_recv()
        copy_of(x_ref, block, core_sem.at[away], partner).wait_send()
    for s in range(chips):

        @pl.when(jnp.logical_and(has_right, chip - s >= 0))
        def _(s=s):
            copy_of(x_ref, dp, right_sem.at[s], right).wait_send()

        @pl.when(jnp.logical_and(has_left, chip + s < chips))
        def _(s=s):
            copy_of(x_ref, dp, left_sem.at[s], left).wait_send()

    local.wait()


def gather_dp(x, cid):
    n = lax.axis_size("dp")
    chips = n // 2
    return pl.pallas_call(
        functools.partial(gather_kernel, chips),
        out_shape=jax.ShapeDtypeStruct((n,) + x.shape, x.dtype),
        in_specs=[pl.BlockSpec(memory_space=pl.ANY)],
        out_specs=pl.BlockSpec(memory_space=pl.ANY),
        scratch_shapes=[
            pltpu.SemaphoreType.DMA((chips,)),
            pltpu.SemaphoreType.DMA((chips,)),
            pltpu.SemaphoreType.DMA((chips,)),
            pltpu.SemaphoreType.DMA((n,)),
            pltpu.SemaphoreType.DMA,
        ],
        compiler_params=pltpu.CompilerParams(collective_id=cid, has_side_effects=True),
        cost_estimate=pl.CostEstimate(
            flops=0, bytes_accessed=n * x.size * 4, transcendentals=0
        ),
        name="gather_dp",
    )(x)


def attend_kernel(heads, page, pages_ref, count_ref, q_ref, kv_ref, qid_ref, kid_ref, out_ref, qbd):
    width = heads * HEAD
    step = pl.program_id(0)
    col = lax.broadcasted_iota(jnp.int32, (page, width), 1) // HEAD
    q = q_ref[...] * jnp.asarray(0.125, BF)
    for h in range(heads):
        qbd[h * page : (h + 1) * page, :] = jnp.where(col == h, q, jnp.zeros_like(q))
    own = jnp.concatenate([qid_ref[...]] * heads, axis=0)
    rows = heads * page
    count = count_ref[step]

    def body(i, carry):
        top, total, acc = carry
        keys, values, ids = [], [], []
        for g in range(GROUP):
            at = i * GROUP + g
            p = pages_ref[step, at]
            block = kv_ref[pl.ds(pl.multiple_of(p * page, page), page), :]
            keys.append(block[:, :width])
            values.append(block[:, width:])
            ids.append(jnp.where(at < count, kid_ref[pl.ds(p, 1), :], -2))
        key = jnp.concatenate(keys, axis=0)
        value = jnp.concatenate(values, axis=0)
        kid = jnp.concatenate(ids, axis=1)
        s = lax.dot_general(qbd[...], key, (((1,), (1,)), ((), ())), preferred_element_type=F32)
        s = jnp.where(own == kid, s, -1e30)
        new_top = jnp.maximum(top, jnp.max(s, axis=1, keepdims=True))
        w = jnp.exp(s - new_top)
        alpha = jnp.exp(top - new_top)
        total = total * alpha + jnp.sum(w, axis=1, keepdims=True)
        acc = acc * alpha + jnp.dot(w.astype(BF), value, preferred_element_type=F32)
        return new_top, total, acc

    init = (
        jnp.full((rows, 1), -1e29, F32),
        jnp.zeros((rows, 1), F32),
        jnp.zeros((rows, width), F32),
    )
    _, total, acc = lax.fori_loop(0, (count + GROUP - 1) // GROUP, body, init)
    acc = acc / total
    result = jnp.zeros((page, width), F32)
    for h in range(heads):
        result = result + jnp.where(col == h, acc[h * page : (h + 1) * page, :], 0.0)
    out_ref[...] = result.astype(BF)


def attend(q, kv, slots, dp):
    rows, width = q.shape
    total_pages, page = slots.shape
    heads = width // HEAD
    own_pages = rows // page
    requests = jnp.arange(-1, 4, dtype=jnp.int32)
    holds = jnp.any(slots[:, :, None] == requests[None, None, :], axis=1)
    own_holds = lax.dynamic_slice_in_dim(holds, dp * own_pages, own_pages, 0)
    need = jnp.any(own_holds[:, None, :] & holds[None, :, :], axis=-1)
    need_int = need.astype(jnp.int32)
    index = jnp.arange(total_pages, dtype=jnp.int32)
    before = (index[:, None] > index[None, :]).astype(jnp.int32)
    place = jnp.sum(need_int[:, None, :] * before[None], axis=-1)
    hit = need[:, :, None] & (place[:, :, None] == index[None, None, :])
    lists = jnp.sum(jnp.where(hit, index[None, :, None], 0), axis=1).astype(jnp.int32)
    lists = jnp.pad(lists, ((0, 0), (0, GROUP)))
    counts = jnp.sum(need_int, axis=1).astype(jnp.int32)
    own_ids = lax.dynamic_slice_in_dim(slots.reshape(-1), dp * rows, rows, 0)[:, None]
    return pl.pallas_call(
        functools.partial(attend_kernel, heads, page),
        out_shape=jax.ShapeDtypeStruct(q.shape, BF),
        grid_spec=pltpu.PrefetchScalarGridSpec(
            num_scalar_prefetch=2,
            grid=(own_pages,),
            in_specs=[
                pl.BlockSpec((page, width), lambda i, *_: (i, 0)),
                pl.BlockSpec(kv.shape, lambda i, *_: (0, 0)),
                pl.BlockSpec((page, 1), lambda i, *_: (i, 0)),
                pl.BlockSpec(slots.shape, lambda i, *_: (0, 0)),
            ],
            out_specs=pl.BlockSpec((page, width), lambda i, *_: (i, 0)),
            scratch_shapes=[pltpu.VMEM((heads * page, width), BF)],
        ),
        compiler_params=pltpu.CompilerParams(vmem_limit_bytes=40 * 2**20),
        cost_estimate=pl.CostEstimate(
            flops=rows * kv.shape[0] * 256 * 4 * 2, bytes_accessed=2 * kv.size,
            transcendentals=rows * kv.shape[0] * heads // 2,
        ),
        name="attend",
    )(lists, counts, q, kv, own_ids, slots)


def norm(value):
    mean = jnp.mean(value, axis=-1, keepdims=True)
    centred = value - mean
    spread = jnp.mean(centred * centred, axis=-1, keepdims=True)
    return centred * lax.rsqrt(spread + 1e-05)


def tail_kernel(
    groups, attn_ref, tok_ref, up_ref, down_ref, wout_ref, live_ref, out_ref,
    heads_buf, part_out, part_in, result,
    attn_send, attn_recv, part_send, part_recv, out_send, out_recv, local_sem,
):
    dp = lax.axis_index("dp")
    me = lax.axis_index("tensor")
    rows = attn_ref.shape[0] // groups
    width = attn_ref.shape[1]

    def span(j):
        return pl.ds(pl.multiple_of(j * rows, rows), rows)

    greet([(None, (dp, lax.rem(me + k, groups))) for k in range(1, groups)])
    own = pltpu.make_async_copy(attn_ref, heads_buf.at[me], local_sem)
    own.start()

    def attn_copy(k, i):
        peer = lax.rem(me + k, groups)
        at = span(lax.rem(peer + 1 + i, groups))
        return pltpu.make_async_remote_copy(
            attn_ref.at[at], heads_buf.at[me, at], attn_send.at[k, i], attn_recv.at[k, i],
            device_id=(dp, peer), device_id_type=MESH,
        )

    def part_copy(i):
        peer = lax.rem(me + 1 + i, groups)
        return pltpu.make_async_remote_copy(
            part_out.at[i], part_in.at[i], part_send.at[i], part_recv.at[i],
            device_id=(dp, peer), device_id_type=MESH,
        )

    def out_copy(k):
        peer = lax.rem(me + k, groups)
        return pltpu.make_async_remote_copy(
            result, out_ref.at[span(me)], out_send.at[k], out_recv.at[k],
            device_id=(dp, peer), device_id_type=MESH,
        )

    for i in range(groups):
        for k in range(1, groups):
            attn_copy(k, i).start()
    own.wait()
    for i in range(groups):
        for k in range(1, groups):
            attn_copy(k, i).wait_recv()
        at = span(lax.rem(me + 1 + i, groups))
        attn = jnp.concatenate([heads_buf[t, at, :] for t in range(groups)], axis=1)
        proj = lax.dot_general(
            attn, wout_ref[...], (((1,), (1,)), ((), ())), preferred_element_type=F32
        )
        first = norm(tok_ref[at, :].astype(F32) + proj).astype(BF)
        hidden = jnp.dot(first, up_ref[...], preferred_element_type=F32)
        inner = (0.5 * hidden * (1.0 + lax.erf(hidden * 0.7071067811865476))).astype(BF)
        part = lax.dot_general(
            inner, down_ref[...], (((1,), (1,)), ((), ())), preferred_element_type=F32
        )
        if i < groups - 1:
            part_out[i] = part.astype(BF)
            part_copy(i).start()
        else:
            total = part
            for n in range(groups - 1):
                part_copy(n).wait_recv()
                total = total + part_in[n].astype(F32)
            value = norm(first.astype(F32) + total) * live_ref[at, :]
            result[...] = value.astype(BF)
    final = pltpu.make_async_copy(result, out_ref.at[span(me)], local_sem)
    final.start()
    for k in range(1, groups):
        out_copy(k).start()
    for k in range(1, groups):
        out_copy(k).wait()
        for i in range(groups):
            attn_copy(k, i).wait_send()
    for n in range(groups - 1):
        part_copy(n).wait_send()
    final.wait()


def tail(attn, tokens, up, down, wout, live, groups, cid):
    rows, width = attn.shape
    wide = tokens.shape[1]
    share = rows // groups
    vmem = pl.BlockSpec(memory_space=pltpu.VMEM)
    return pl.pallas_call(
        functools.partial(tail_kernel, groups),
        out_shape=jax.ShapeDtypeStruct(tokens.shape, BF),
        in_specs=[vmem] * 6,
        out_specs=pl.BlockSpec(memory_space=pl.ANY),
        scratch_shapes=[
            pltpu.VMEM((groups, rows, width), BF),
            pltpu.VMEM((groups - 1, share, wide), BF),
            pltpu.VMEM((groups - 1, share, wide), BF),
            pltpu.VMEM((share, wide), BF),
            pltpu.SemaphoreType.DMA((groups, groups)),
            pltpu.SemaphoreType.DMA((groups, groups)),
            pltpu.SemaphoreType.DMA((groups,)),
            pltpu.SemaphoreType.DMA((groups,)),
            pltpu.SemaphoreType.DMA((groups,)),
            pltpu.SemaphoreType.DMA((groups,)),
            pltpu.SemaphoreType.DMA,
        ],
        compiler_params=pltpu.CompilerParams(
            collective_id=cid, has_side_effects=True, vmem_limit_bytes=48 * 2**20
        ),
        name="tail",
    )(attn, tokens, up, down, wout, live)


def shards(tokens, w_qkv, w_out, w_up, w_down, slot_request):
    groups = lax.axis_size("tensor")
    dp = lax.axis_index("dp")
    slab, wide = w_qkv.shape[0], tokens.shape[1]
    heads = wide // HEAD // groups
    width = heads * HEAD
    rows = tokens.shape[0]

    qkv_w = w_qkv.astype(BF).reshape(slab, groups, heads, 3, HEAD)
    qkv_w = jnp.transpose(qkv_w, (1, 0, 3, 2, 4)).reshape(groups, slab, 3 * width)
    up_w = jnp.transpose(w_up.astype(BF).reshape(slab, groups, -1), (1, 0, 2))
    down_w = jnp.transpose(w_down.astype(BF).reshape(groups, -1, slab), (0, 2, 1))
    out_w = jnp.broadcast_to(jnp.transpose(w_out.astype(BF))[None], (groups, slab, wide))
    packed = jnp.concatenate([qkv_w, up_w, down_w, out_w], axis=2)
    cut = 3 * width
    ff = up_w.shape[2]
    mine = exchange(packed, groups, 0).reshape(groups * slab, -1)
    rest = lax.all_gather(mine[:, cut:], "dp", axis=0, tiled=True)
    qkv_block = gather_dp(mine[:, :cut], 1).reshape(wide, cut)
    qkv = jnp.dot(tokens, qkv_block, preferred_element_type=F32).astype(BF)
    kv = gather_dp(qkv[:, width:], 2).reshape(-1, 2 * width)
    attn = attend(qkv[:, :width], kv, slot_request, dp)
    own_ids = lax.dynamic_slice_in_dim(slot_request.reshape(-1), dp * rows, rows, 0)
    live = (own_ids >= 0).astype(F32)[:, None]
    return tail(
        attn, tokens, rest[:, :ff], rest[:, ff : 2 * ff], rest[:, 2 * ff :], live, groups, 3
    )


def solution(mesh):
    in_specs = (
        P("dp", None),
        P(("dp", "tensor"), None),
        P(None, ("dp", "tensor")),
        P(("dp", "tensor"), None),
        P(None, ("dp", "tensor")),
        P(),
    )
    out_specs = P("dp", None)
    return jax.shard_map(shards, mesh=mesh, in_specs=in_specs, out_specs=out_specs, check_vma=False)
```

time: 615 us -> 256 us (0.42)
  waiting for transfers between devices: 419 us -> 0.04 us
  Pallas kernels: 0 us -> 220 us
  matrix products: 122 us -> 2.83 us
  other arithmetic: 35.1 us -> 5.01 us
  local copies, waits for them, and re-layouts: 22.8 us -> 15.7 us
    all_gather x6 -> x1, waiting for transfers between devices: 301 us -> 0.02 us  [shards(): rest = lax.all_gather(mine[:, cut:], 'dp', axis=0, tiled=True)]
    pallas_call x0 -> x5, Pallas kernels: none -> 220 us  [the longest x2 117 us: gather_dp(): pl.pallas_call(functools.partial(gather_kernel, chips), out_shape=jax.Sha...]
    dot_general x19 -> x1, matrix products: 122 us -> 2.83 us  [shards(): qkv = jnp.dot(tokens, qkv_block, preferred_element_type=F32).astype(BF)]
    psum x2 -> x0, waiting for transfers between devices: 118 us -> none  [the longest x1 59.7 us: shards(): lax.psum(jnp.dot(inner, down_block, preferred_element_type=jnp.float32).a...]
    reduce_sum x12 -> x3, other arithmetic: 23.9 us -> 0.45 us  [the longest x1 0.17 us: attend(): place = jnp.sum(need_int[:, None, :] * before[None], axis=-1)]
    dynamic_slice x32 -> x1, local copies, waits for them, and re-layouts: 12.3 us -> 0.08 us  [attend(): own_holds = lax.dynamic_slice_in_dim(holds, dp * own_pages, own_pages, 0)]
    slice x1 -> x5, local copies, waits for them, and re-layouts: 0.98 us -> 10.4 us  [the longest x1 5.62 us: shards(): rest[:, 2 * ff:]]
    all_gather x2 -> x0, local copies, waits for them, and re-layouts: 9.37 us -> none  [the longest x1 4.72 us: shards(): value_piece = lax.all_gather(value_rows, 'dp', axis=0, tiled=True)]
  transfers between devices with their start and end apart: 8 -> 1, of which waited for: 7 -> 0; matrix products, arithmetic and copies ran while one was open for 25% -> 3% of each run, Pallas kernels for 0% -> 59%
where the time goes in v1:
time: 256 us; the launch traced here: 257 us
  Pallas kernels  220 us (86%)
  local copies, waits for them, and re-layouts  15.7 us (6%)
  between operations  13.6 us (5%)
  other arithmetic  5.01 us (2%)
  matrix products  2.83 us (1%)
    pallas_call x2, Pallas kernels, gather_dp(): pl.pallas_call(functools.partial(gather_kernel, chips), out_shape=jax.Sha...  117 us
    pallas_call x1, Pallas kernels, tail(): pl.pallas_call(functools.partial(tail_kernel, groups), out_shape=jax.Shap...  52 us
    pallas_call x1, Pallas kernels, attend(): pl.pallas_call(functools.partial(attend_kernel, heads, page), out_shape=j...  34.4 us
    pallas_call x1, Pallas kernels, exchange(): pl.pallas_call(functools.partial(exchange_kernel, groups), out_shape=jax....  15.8 us
    slice x1, local copies, waits for them, and re-layouts, shards(): rest[:, 2 * ff:]  5.62 us
  transfers between devices with their start and end apart: 1, of which 0 were waited for; matrix products, arithmetic and copies ran while one was open for 3% of the time, Pallas kernels for 59%

profile of v1, /device:TPU:0, one launch (start us, length us, event | category | flops | bytes accessed | tf_op | source)
XLA Modules:
  0.0 256.8 jit_solution(15520648656791730757)
XLA Ops:
  6.5 0.0 copy-start.3
  6.5 0.0 all-gather.2.cloned.1.call-start
  6.5 1.0 convert_bitcast_fusion
  7.5 1.1 convert_element_type.37
  8.6 1.1 convert_element_type.36
  9.6 0.0 copy-done.3
  9.7 0.4 reshape.51
  10.1 0.2 copy.15
  10.3 0.3 reshape.52
  10.6 1.0 pad_maximum_fusion.x_ref
  11.7 15.8 %exchange.1 = bf16[4,32,3840]{2,1,0:T(8,128)(2,1)} custom-call(bf16[4,32,3840]{2,1,0:T(8,128)(2,1)} %pad_maximum_fusion.x_ref), custom_call_target="tpu_custom_call" | custom-call | tf_op jit(solution)/shard_map/exchange/pallas_call | solution.py:53
  27.5 0.0 copy-start.1
  27.5 2.2 slice.31
  29.7 0.0 all-gather.2.cloned.1.call-update
  29.8 1.6 slice.28.x_ref
  31.4 44.8 %gather_dp.2 = bf16[8,128,768]{2,1,0:T(8,128)(2,1)} custom-call(bf16[128,768]{1,0:T(8,128)(2,1)} %slice.28.x_ref), custom_call_target="tpu_custom_call" | custom-call | bytes 3145728 | tf_op jit(solution)/shard_map/gather_dp/pallas_call | solution.py:133
  76.2 0.0 copy-done.1
  76.2 2.8 %fusion = bf16[768,768]{1,0:T(8,128)(2,1)S(1)} fusion(bf16[768,1024]{1,0:T(8,128)(2,1)S(1)} %copy-done.1, bf16[1024,768]{1,0:T(8,128)(2,1)} %bitcast.26), kind=kOutput, calls=%fused_computation.1 | convolution fusion | flops 1208549376 | bytes 4325376 | tf_op jit(solution)/shard_map/dot_general | solution.py:377
  79.0 0.0 copy-start.2
  79.1 0.9 slice.30.x_ref
  80.0 0.0 copy-done.2
  80.0 0.2 compare_reduce_fusion
  80.3 0.1 constant_dynamic-slice_fusion
  80.3 0.1 and_reduce_fusion
  80.5 0.2 multiply_reduce_fusion
  80.6 0.2 select_reduce_fusion
  80.8 72.6 %gather_dp.3 = bf16[8,768,512]{2,1,0:T(8,128)(2,1)} custom-call(bf16[768,512]{1,0:T(8,128)(2,1)} %slice.30.x_ref), custom_call_target="tpu_custom_call" | custom-call | bytes 12582912 | tf_op jit(solution)/shard_map/gather_dp/pallas_call | solution.py:133
  153.4 0.1 compare_convert_fusion
  153.5 0.2 broadcast_in_dim.45.qid_ref
  153.7 0.2 reshape.60.live_ref
  153.9 0.1 convert_reduce_fusion.count_ref
  154.0 0.0 copy-start
  154.0 2.8 %copy-done = bf16[8,768,512]{2,1,0:T(8,128)(2,1)S(1)} copy-done((bf16[8,768,512]{2,1,0:T(8,128)(2,1)S(1)}, bf16[8,768,512]{2,1,0:T(8,128)(2,1)}, u32[]{:S(2)}) %copy-start) | copy-done | bytes 6291480
  156.8 34.4 %attend.1.attn_ref = bf16[768,256]{1,0:T(8,128)(2,1)S(1)} custom-call(s32[6,52]{1,0:T(8,128)S(1)} %pad.4.pages_ref, s32[6]{0:T(128)S(1)} %convert_reduce_fusion.count_ref, bf16[768,256]{1,0:T(8,128)(2,1)S(1)} %slice.29.q_ref, bf16[6144,512]{1,0:T(8,128)(2,1)S(1)} %bitcast.21, s32[768,1]{1,0:T(8,128)S(1)} %broadcast_in_dim.45.qid_ref, s32[48,128]{1,0:T(8,128)S(1)} %copy-done.2), custom_call_target="tpu_custom_call" | custom-call | flops 9663676416 | bytes 6291456 | tf_op jit(solution)/shard_map/attend/pallas_call | solution.py:217
  191.2 0.0 all-gather.2.cloned.1.call-done
  191.2 5.6 %fusion.3 = (bf16[1024,1024]{1,0:T(8,128)(2,1)}, bf16[1024,1024]{1,0:T(8,128)(2,1)}, bf16[1024,1024]{1,0:T(8,128)(2,1)S(1)}) fusion(bf16[1024,3072]{1,0:T(8,128)(2,1)} %all-gather.2.cloned.1.call-done), kind=kLoop, calls=%fused_computation.18 | loop fusion | bytes 12582912 | tf_op jit(solution)/shard_map/slice | solution.py:383
  196.8 52.0 %tail.1 = bf16[768,1024]{1,0:T(8,128)(2,1)S(1)} custom-call(bf16[768,256]{1,0:T(8,128)(2,1)S(1)} %attend.1.attn_ref, bf16[768,1024]{1,0:T(8,128)(2,1)S(1)} %copy-done.1, bf16[1024,1024]{1,0:T(8,128)(2,1)S(1)} %get-tuple-element.9.up_ref, bf16[1024,1024]{1,0:T(8,128)(2,1)} %get-tuple-element.8.down_ref, bf16[1024,1024]{1,0:T(8,128)(2,1)} %get-tuple-element.7.wout_ref, ...), custom_call_target="tpu_custom_call" | custom-call | tf_op jit(solution)/shard_map/tail/pallas_call | solution.py:333
  248.8 1.1 copy.27
  (8 shorter events, 0.1 us)
Async XLA Ops:
  6.5 3.1 %copy-start.3 = (f32[32,3072]{1,0:T(8,128)S(1)}, f32[32,3072]{1,0:T(8,128)}, u32[]{:S(2)}) copy-start(f32[32,3072]{1,0:T(8,128)} %param.7) | copy-start | bytes 1179652
  6.5 184.6 %all-gather.2.cloned.1.call-start = ((), (), s32[]{:S(2)}) async-start(), calls=%async_computation | async-start | bytes 7077888 | tf_op jit(solution)/shard_map/all_gather | solution.py:375
  27.5 48.7 %copy-start.1 = (bf16[768,1024]{1,0:T(8,128)(2,1)S(1)}, bf16[768,1024]{1,0:T(8,128)(2,1)}, u32[]{:S(2)}) copy-start(bf16[768,1024]{1,0:T(8,128)(2,1)} %tok_ref.1) | copy-start | bytes 4718596
  79.0 1.0 copy-start.2
  154.0 2.8 %copy-start = (bf16[8,768,512]{2,1,0:T(8,128)(2,1)S(1)}, bf16[8,768,512]{2,1,0:T(8,128)(2,1)}, u32[]{:S(2)}) copy-start(bf16[8,768,512]{2,1,0:T(8,128)(2,1)} %gather_dp.3) | copy-start | bytes 18874372
Sparse Core Ops, SparseCore 0:
  29.9 79.8 all-gather.1

commit v2 on v1

v2 whole, which is shorter than its diff:
```python
import functools

import jax
import jax.numpy as jnp
from jax import lax
from jax.experimental import pallas as pl
from jax.experimental.pallas import tpu as pltpu
from jax.sharding import PartitionSpec as P

HEAD = 64
MESH = pl.DeviceIdType.MESH
GROUP = 4
BF = jnp.bfloat16
F32 = jnp.float32


def greet(targets):
    barrier = pltpu.get_barrier_semaphore()
    for cond, dev in targets:
        if cond is None:
            pl.semaphore_signal(barrier, inc=1, device_id=dev, device_id_type=MESH)
        else:

            @pl.when(cond)
            def _(dev=dev):
                pl.semaphore_signal(barrier, inc=1, device_id=dev, device_id_type=MESH)

    count = sum(1 if cond is None else jnp.where(cond, 1, 0) for cond, _ in targets)
    pl.semaphore_wait(barrier, count)


def exchange_kernel(groups, count, *refs):
    x_refs, out_refs = refs[:count], refs[count : 2 * count]
    send_sem, recv_sem, local_sem = refs[2 * count :]
    dp = lax.axis_index("dp")
    me = lax.axis_index("tensor")
    greet([(None, (dp, lax.rem(me + k, groups))) for k in range(1, groups)])
    sends = []
    for n in range(count):
        for k in range(1, groups):
            peer = lax.rem(me + k, groups)
            copy = pltpu.make_async_remote_copy(
                x_refs[n].at[peer], out_refs[n].at[me], send_sem.at[n, k], recv_sem.at[n, k],
                device_id=(dp, peer), device_id_type=MESH,
            )
            copy.start()
            sends.append(copy)
        local = pltpu.make_async_copy(x_refs[n].at[me], out_refs[n].at[me], local_sem.at[n])
        local.start()
        sends.append(local)
    for copy in sends:
        copy.wait()


def exchange(arrays, groups, cid):
    count = len(arrays)
    hbm = pl.BlockSpec(memory_space=pl.ANY)
    return pl.pallas_call(
        functools.partial(exchange_kernel, groups, count),
        out_shape=[jax.ShapeDtypeStruct(x.shape, x.dtype) for x in arrays],
        in_specs=[hbm] * count,
        out_specs=[hbm] * count,
        scratch_shapes=[
            pltpu.SemaphoreType.DMA((count, groups)),
            pltpu.SemaphoreType.DMA((count, groups)),
            pltpu.SemaphoreType.DMA((count,)),
        ],
        compiler_params=pltpu.CompilerParams(collective_id=cid, has_side_effects=True),
        name="exchange",
    )(*arrays)


def gather_kernel(chips, count, cols, groups, *refs):
    total = count + (1 if groups else 0)
    x_refs, out_refs = list(refs[:total]), refs[total : 2 * total]
    right_sem, left_sem, core_sem, recv_sem, local_sem, side_send, side_recv = refs[2 * total :]
    dp = lax.axis_index("dp")
    tensor = lax.axis_index("tensor")
    chip, core = dp // 2, lax.rem(dp, 2)
    other = 1 - core
    partner = (2 * chip + other, tensor)
    has_right, has_left = chip + 1 < chips, chip > 0
    right = (2 * jnp.minimum(chip + 1, chips - 1) + core, tensor)
    left = (2 * jnp.maximum(chip - 1, 0) + core, tensor)
    peers = [(dp, lax.rem(tensor + k, groups)) for k in range(1, groups)] if groups else []
    greet(
        [(None, partner), (has_right, right), (has_left, left)]
        + [(None, peer) for peer in peers]
    )
    if cols is not None:
        x_refs[0] = x_refs[0].at[:, cols[0] : cols[1]]

    def copy_of(n, source, block, send, device):
        return pltpu.make_async_remote_copy(
            source, out_refs[n].at[block], send, recv_sem.at[n, block],
            device_id=device, device_id_type=MESH,
        )

    for n in range(count):

        @pl.when(has_right)
        def _(n=n):
            copy_of(n, x_refs[n], dp, right_sem.at[n, 0], right).start()

        @pl.when(has_left)
        def _(n=n):
            copy_of(n, x_refs[n], dp, left_sem.at[n, 0], left).start()

        copy_of(n, x_refs[n], dp, core_sem.at[n, chip], partner).start()
    for n in range(count):
        pltpu.make_async_copy(x_refs[n], out_refs[n].at[dp], local_sem.at[n]).start()
    side = []
    for k, peer in enumerate(peers):
        side.append(
            pltpu.make_async_remote_copy(
                x_refs[count], out_refs[count].at[tensor], side_send.at[k], side_recv.at[k],
                device_id=peer, device_id_type=MESH,
            )
        )
    if groups:
        side.append(
            pltpu.make_async_copy(
                x_refs[count], out_refs[count].at[tensor], local_sem.at[count]
            )
        )
    for copy in side:
        copy.start()
    for s in range(1, chips):
        for n in range(count):
            for away, has_next, sems, following in (
                (chip - s, has_right, right_sem, right),
                (chip + s, has_left, left_sem, left),
            ):

                @pl.when(jnp.logical_and(away >= 0, away < chips))
                def _(n=n, away=away, has_next=has_next, sems=sems, following=following, s=s):
                    block = 2 * away + core
                    here = out_refs[n].at[block]
                    copy_of(n, here, block, core_sem.at[n, away], partner).wait_recv()

                    @pl.when(has_next)
                    def _():
                        copy_of(n, here, block, sems.at[n, s], following).start()

                    copy_of(n, here, block, core_sem.at[n, away], partner).start()

    for n in range(count):
        for away in range(chips):
            block = 2 * away + other
            copy_of(n, x_refs[n], block, core_sem.at[n, away], partner).wait()
        for s in range(chips):

            @pl.when(jnp.logical_and(has_right, chip - s >= 0))
            def _(n=n, s=s):
                copy_of(n, x_refs[n], dp, right_sem.at[n, s], right).wait_send()

            @pl.when(jnp.logical_and(has_left, chip + s < chips))
            def _(n=n, s=s):
                copy_of(n, x_refs[n], dp, left_sem.at[n, s], left).wait_send()

        pltpu.make_async_copy(x_refs[n], out_refs[n].at[dp], local_sem.at[n]).wait()
    for copy in side:
        copy.wait()


def gather_dp(arrays, cid, cols=None, side=None, groups=0):
    n = lax.axis_size("dp")
    chips = n // 2
    count = len(arrays)
    shapes = [x.shape for x in arrays]
    if cols is not None:
        shapes[0] = (shapes[0][0], cols[1] - cols[0])
    shapes = [(n,) + shape for shape in shapes]
    if side is not None:
        arrays = arrays + [side]
        shapes.append((groups,) + side.shape)
    hbm = pl.BlockSpec(memory_space=pl.ANY)
    return pl.pallas_call(
        functools.partial(gather_kernel, chips, count, cols, groups),
        out_shape=[jax.ShapeDtypeStruct(shape, BF) for shape in shapes],
        in_specs=[hbm] * len(shapes),
        out_specs=[hbm] * len(shapes),
        scratch_shapes=[
            pltpu.SemaphoreType.DMA((count, chips)),
            pltpu.SemaphoreType.DMA((count, chips)),
            pltpu.SemaphoreType.DMA((count, chips)),
            pltpu.SemaphoreType.DMA((count, n)),
            pltpu.SemaphoreType.DMA((count + 1,)),
            pltpu.SemaphoreType.DMA((max(groups, 1),)),
            pltpu.SemaphoreType.DMA((max(groups, 1),)),
        ],
        compiler_params=pltpu.CompilerParams(collective_id=cid, has_side_effects=True),
        cost_estimate=pl.CostEstimate(
            flops=0, bytes_accessed=n * arrays[0].size * 4, transcendentals=0
        ),
        name="gather_dp",
    )(*arrays)


def attend_kernel(heads, page, pages_ref, count_ref, q_ref, kv_ref, qid_ref, kid_ref, out_ref, qbd):
    width = heads * HEAD
    pair = 2 * HEAD
    step = pl.program_id(0)
    low = lax.broadcasted_iota(jnp.int32, (page, pair), 1) < HEAD
    q = q_ref[...] * jnp.asarray(0.125, BF)
    zero = jnp.zeros((page, pair), BF)
    for h in range(heads // 2):
        both = q[:, h * pair : (h + 1) * pair]
        qbd[h, :page, :] = jnp.where(low, both, zero)
        qbd[h, page:, :] = jnp.where(low, zero, both)
    own = jnp.concatenate([qid_ref[...]] * 2, axis=0)
    rows = 2 * page
    count = count_ref[step]

    def body(i, carry):
        blocks, ids = [], []
        for g in range(GROUP):
            at = i * GROUP + g
            p = pages_ref[step, at]
            blocks.append(kv_ref[pl.ds(pl.multiple_of(p * page, page), page), :])
            ids.append(jnp.where(at < count, kid_ref[pl.ds(p, 1), :], -2))
        block = jnp.concatenate(blocks, axis=0)
        kid = jnp.concatenate(ids, axis=1)
        allowed = own == kid
        after = []
        scores = [
            lax.dot_general(
                qbd[h], block[:, h * pair : (h + 1) * pair],
                (((1,), (1,)), ((), ())), preferred_element_type=F32,
            )
            for h in range(heads // 2)
        ]
        for h in range(heads // 2):
            top, total, acc = carry[h]
            value = block[:, width + h * pair : width + (h + 1) * pair]
            s = jnp.where(allowed, scores[h], -1e30)
            new_top = jnp.maximum(top, jnp.max(s, axis=1, keepdims=True))
            w = jnp.exp(s - new_top)
            alpha = jnp.exp(top - new_top)
            total = total * alpha + jnp.sum(w, axis=1, keepdims=True)
            acc = acc * alpha + jnp.dot(w.astype(BF), value, preferred_element_type=F32)
            after.append((new_top, total, acc))
        return tuple(after)

    init = (
        jnp.full((rows, 1), -1e29, F32),
        jnp.zeros((rows, 1), F32),
        jnp.zeros((rows, pair), F32),
    )
    final = lax.fori_loop(0, (count + GROUP - 1) // GROUP, body, (init,) * (heads // 2))
    for h in range(heads // 2):
        _, total, acc = final[h]
        acc = (acc / total).astype(BF)
        out_ref[:, h * pair : (h + 1) * pair] = jnp.where(low, acc[:page], acc[page:])


def attend(q, kv, slots, dp):
    rows, width = q.shape[0], kv.shape[1] // 2
    total_pages, page = slots.shape
    heads = width // HEAD
    own_pages = rows // page
    requests = jnp.arange(-1, 4, dtype=jnp.int32)
    holds = jnp.any(slots[:, :, None] == requests[None, None, :], axis=1)
    own_holds = lax.dynamic_slice_in_dim(holds, dp * own_pages, own_pages, 0)
    need = jnp.any(own_holds[:, None, :] & holds[None, :, :], axis=-1)
    need_int = need.astype(jnp.int32)
    index = jnp.arange(total_pages, dtype=jnp.int32)
    before = (index[:, None] > index[None, :]).astype(jnp.int32)
    place = jnp.sum(need_int[:, None, :] * before[None], axis=-1)
    hit = need[:, :, None] & (place[:, :, None] == index[None, None, :])
    lists = jnp.sum(jnp.where(hit, index[None, :, None], 0), axis=1).astype(jnp.int32)
    lists = jnp.pad(lists, ((0, 0), (0, GROUP)))
    counts = jnp.sum(need_int, axis=1).astype(jnp.int32)
    own_ids = lax.dynamic_slice_in_dim(slots.reshape(-1), dp * rows, rows, 0)[:, None]
    return pl.pallas_call(
        functools.partial(attend_kernel, heads, page),
        out_shape=jax.ShapeDtypeStruct((rows, width), BF),
        grid_spec=pltpu.PrefetchScalarGridSpec(
            num_scalar_prefetch=2,
            grid=(own_pages,),
            in_specs=[
                pl.BlockSpec((page, width), lambda i, *_: (i, 0)),
                pl.BlockSpec(kv.shape, lambda i, *_: (0, 0)),
                pl.BlockSpec((page, 1), lambda i, *_: (i, 0)),
                pl.BlockSpec(slots.shape, lambda i, *_: (0, 0)),
            ],
            out_specs=pl.BlockSpec((page, width), lambda i, *_: (i, 0)),
            scratch_shapes=[pltpu.VMEM((heads // 2, 2 * page, 2 * HEAD), BF)],
        ),
        compiler_params=pltpu.CompilerParams(vmem_limit_bytes=40 * 2**20),
        cost_estimate=pl.CostEstimate(
            flops=rows * kv.shape[0] * 256 * 4 * 2, bytes_accessed=2 * kv.size,
            transcendentals=rows * kv.shape[0] * heads // 2,
        ),
        name="attend",
    )(lists, counts, q, kv, own_ids, slots)


def norm(value):
    mean = jnp.mean(value, axis=-1, keepdims=True)
    centred = value - mean
    spread = jnp.mean(centred * centred, axis=-1, keepdims=True)
    return centred * lax.rsqrt(spread + 1e-05)


def tail_kernel(
    groups, attn_ref, tok_ref, ffw_ref, wout_ref, live_ref, out_ref,
    heads_buf, wout, part_out, part_in, result,
    attn_send, attn_recv, part_send, part_recv, out_send, out_recv, local_sem,
):
    dp = lax.axis_index("dp")
    me = lax.axis_index("tensor")
    rows = attn_ref.shape[0] // groups
    width = attn_ref.shape[1]
    ff = ffw_ref.shape[1] // 2

    def span(j):
        return pl.ds(pl.multiple_of(j * rows, rows), rows)

    greet([(None, (dp, lax.rem(me + k, groups))) for k in range(1, groups)])
    own = pltpu.make_async_copy(attn_ref, heads_buf.at[me], local_sem)
    own.start()

    def attn_copy(k, i):
        peer = lax.rem(me + k, groups)
        at = span(lax.rem(peer + 1 + i, groups))
        return pltpu.make_async_remote_copy(
            attn_ref.at[at], heads_buf.at[me, at], attn_send.at[k, i], attn_recv.at[k, i],
            device_id=(dp, peer), device_id_type=MESH,
        )

    def part_copy(i):
        peer = lax.rem(me + 1 + i, groups)
        return pltpu.make_async_remote_copy(
            part_out.at[i], part_in.at[i], part_send.at[i], part_recv.at[i],
            device_id=(dp, peer), device_id_type=MESH,
        )

    def out_copy(k):
        peer = lax.rem(me + k, groups)
        return pltpu.make_async_remote_copy(
            result, out_ref.at[span(me)], out_send.at[k], out_recv.at[k],
            device_id=(dp, peer), device_id_type=MESH,
        )

    for i in range(groups):
        for k in range(1, groups):
            attn_copy(k, i).start()
    for t in range(groups):
        wout[:, t * width : (t + 1) * width] = wout_ref[t]
    own.wait()
    for i in range(groups):
        for k in range(1, groups):
            attn_copy(k, i).wait_recv()
        at = span(lax.rem(me + 1 + i, groups))
        attn = jnp.concatenate([heads_buf[t, at, :] for t in range(groups)], axis=1)
        proj = lax.dot_general(
            attn, wout[...], (((1,), (1,)), ((), ())), preferred_element_type=F32
        )
        first = norm(tok_ref[at, :].astype(F32) + proj).astype(BF)
        hidden = jnp.dot(first, ffw_ref[:, :ff], preferred_element_type=F32)
        inner = (0.5 * hidden * (1.0 + lax.erf(hidden * 0.7071067811865476))).astype(BF)
        part = lax.dot_general(
            inner, ffw_ref[:, ff:], (((1,), (1,)), ((), ())), preferred_element_type=F32
        )
        if i < groups - 1:
            part_out[i] = part.astype(BF)
            part_copy(i).start()
        else:
            total = part
            for n in range(groups - 1):
                part_copy(n).wait_recv()
                total = total + part_in[n].astype(F32)
            value = norm(first.astype(F32) + total) * live_ref[at, :]
            result[...] = value.astype(BF)
    final = pltpu.make_async_copy(result, out_ref.at[span(me)], local_sem)
    final.start()
    for k in range(1, groups):
        out_copy(k).start()
    for k in range(1, groups):
        out_copy(k).wait()
        for i in range(groups):
            attn_copy(k, i).wait_send()
    for n in range(groups - 1):
        part_copy(n).wait_send()
    final.wait()


def tail(attn, tokens, ffw, wout, live, groups, cid):
    rows, width = attn.shape
    wide = tokens.shape[1]
    share = rows // groups
    vmem = pl.BlockSpec(memory_space=pltpu.VMEM)
    return pl.pallas_call(
        functools.partial(tail_kernel, groups),
        out_shape=jax.ShapeDtypeStruct(tokens.shape, BF),
        in_specs=[vmem] * 5,
        out_specs=pl.BlockSpec(memory_space=pl.ANY),
        scratch_shapes=[
            pltpu.VMEM((groups, rows, width), BF),
            pltpu.VMEM((wide, wide), BF),
            pltpu.VMEM((groups - 1, share, wide), BF),
            pltpu.VMEM((groups - 1, share, wide), BF),
            pltpu.VMEM((share, wide), BF),
            pltpu.SemaphoreType.DMA((groups, groups)),
            pltpu.SemaphoreType.DMA((groups, groups)),
            pltpu.SemaphoreType.DMA((groups,)),
            pltpu.SemaphoreType.DMA((groups,)),
            pltpu.SemaphoreType.DMA((groups,)),
            pltpu.SemaphoreType.DMA((groups,)),
            pltpu.SemaphoreType.DMA,
        ],
        compiler_params=pltpu.CompilerParams(
            collective_id=cid, has_side_effects=True, vmem_limit_bytes=48 * 2**20
        ),
        name="tail",
    )(attn, tokens, ffw, wout, live)


def shards(tokens, w_qkv, w_out, w_up, w_down, slot_request):
    groups = lax.axis_size("tensor")
    dp = lax.axis_index("dp")
    slab, wide = w_qkv.shape[0], tokens.shape[1]
    heads = wide // HEAD // groups
    width = heads * HEAD
    rows = tokens.shape[0]

    qkv_w = w_qkv.astype(BF).reshape(slab, groups, heads, 3, HEAD)
    qkv_w = jnp.transpose(qkv_w, (1, 0, 3, 2, 4)).reshape(groups, slab, 3 * width)
    up_w = jnp.transpose(w_up.astype(BF).reshape(slab, groups, -1), (1, 0, 2))
    down_w = jnp.transpose(w_down.astype(BF).reshape(groups, -1, slab), (0, 2, 1))
    ffw = jnp.concatenate([up_w, down_w], axis=2)
    out_w = jnp.transpose(w_out.astype(BF).reshape(groups, width, slab), (0, 2, 1))
    mine = exchange([qkv_w, out_w, ffw], groups, 0)
    mine = [x.reshape(groups * slab, x.shape[2]) for x in mine]
    qkv_block, out_block = gather_dp(mine[:2], 1)
    late, qkv_block = lax.optimization_barrier((mine[2], qkv_block))
    ffw = lax.all_gather(late, "dp", axis=0, tiled=True)
    qkv = jnp.dot(
        tokens, qkv_block.reshape(wide, 3 * width), preferred_element_type=F32
    ).astype(BF)
    kv, wout = gather_dp(
        [qkv], 2, cols=(width, 3 * width), side=out_block.reshape(wide, width), groups=groups
    )
    kv = kv.reshape(-1, 2 * width)
    attn = attend(qkv, kv, slot_request, dp)
    own_ids = lax.dynamic_slice_in_dim(slot_request.reshape(-1), dp * rows, rows, 0)
    live = (own_ids >= 0).astype(F32)[:, None]
    return tail(attn, tokens, ffw, wout, live, groups, 3)


def solution(mesh):
    in_specs = (
        P("dp", None),
        P(("dp", "tensor"), None),
        P(None, ("dp", "tensor")),
        P(("dp", "tensor"), None),
        P(None, ("dp", "tensor")),
        P(),
    )
    out_specs = P("dp", None)
    return jax.shard_map(shards, mesh=mesh, in_specs=in_specs, out_specs=out_specs, check_vma=False)
```

time: 256 us -> 235 us (0.918); the launches traced: 257 us -> 232 us
  Pallas kernels: 220 us -> 202 us
  local copies, waits for them, and re-layouts: 15.7 us -> 9.22 us
    pallas_call x1, Pallas kernels: 34.4 us -> 18.9 us  [attend(): pl.pallas_call(functools.partial(attend_kernel, heads, page), out_shape=j...]
    slice x5 -> x0, local copies, waits for them, and re-layouts: 10.4 us -> none  [the longest x1 5.62 us: shards(): rest[:, 2 * ff:]]
    pallas_call x3, Pallas kernels: 133 us -> 128 us  [the longest x2 114 us: gather_dp(): pl.pallas_call(functools.partial(gather_kernel, chips, count, cols, group...]
    pallas_call x1, Pallas kernels: 52 us -> 54.8 us  [tail(): pl.pallas_call(functools.partial(tail_kernel, groups), out_shape=jax.Shap...]
    unnamed x9 -> x17, local copies, waits for them, and re-layouts: 3.95 us -> 6.63 us
  transfers between devices with their start and end apart: 1 -> 1, of which waited for: 0 -> 0; matrix products, arithmetic and copies ran while one was open for 3% -> 2% of each run, Pallas kernels for 59% -> 48%
where the time goes in v2:
time: 235 us; the launch traced here: 232 us
  Pallas kernels  202 us (86%)
  between operations  13.6 us (6%)
  local copies, waits for them, and re-layouts  9.22 us (4%)
  other arithmetic  3.92 us (2%)
  matrix products  3.8 us (2%)
    pallas_call x2, Pallas kernels, gather_dp(): pl.pallas_call(functools.partial(gather_kernel, chips, count, cols, group...  114 us
    pallas_call x1, Pallas kernels, tail(): pl.pallas_call(functools.partial(tail_kernel, groups), out_shape=jax.Shap...  54.8 us
    pallas_call x1, Pallas kernels, attend(): pl.pallas_call(functools.partial(attend_kernel, heads, page), out_shape=j...  18.9 us
    pallas_call x1, Pallas kernels, exchange(): pl.pallas_call(functools.partial(exchange_kernel, groups, count), out_sha...  13.8 us
    unnamed x17, local copies, waits for them, and re-layouts  6.63 us
  transfers between devices with their start and end apart: 1, of which 0 were waited for; matrix products, arithmetic and copies ran while one was open for 2% of the time, Pallas kernels for 48%

profile of v2, /device:TPU:0, one launch (start us, length us, event | category | flops | bytes accessed | tf_op | source)
XLA Modules:
  0.0 232.3 jit_solution(13858501126641713933)
XLA Ops:
  6.5 0.0 copy-start.6
  6.5 0.0 all-gather.2.cloned.1.call-start
  6.5 1.1 convert_element_type.36
  7.7 1.1 convert_element_type.37
  8.7 0.0 copy-done.6
  8.7 0.0 copy-start.7
  8.8 0.4 reshape.62
  9.2 0.2 copy.16
  9.4 0.9 reshape.63.refs_0_
  10.3 0.0 copy-done.7
  10.3 0.6 copy.30
  11.0 0.0 copy-start.4
  11.0 0.0 copy-start.1
  11.0 0.8 pad_maximum_fusion.refs_2_
  11.9 13.8 %exchange.1 = (bf16[4,32,768]{2,1,0:T(8,128)(2,1)}, bf16[4,32,256]{2,1,0:T(8,128)(2,1)}, bf16[4,32,2048]{2,1,0:T(8,128)(2,1)}) custom-call(bf16[4,32,768]{2,1,0:T(8,128)(2,1)} %reshape.63.refs_0_, bf16[4,32,256]{2,1,0:T(8,128)(2,1)} %bitcast.36, bf16[4,32,2048]{2,1,0:T(8,128)(2,1)} %pad_maximum_fusion.refs_2_), custom_call_target="tpu_custom_call" | custom-call | tf_op jit(solution)/shard_map/exchange/pallas_call | solution.py:58
  25.7 22.6 %gather_dp.2 = (bf16[8,128,768]{2,1,0:T(8,128)(2,1)}, bf16[8,128,256]{2,1,0:T(8,128)(2,1)}) custom-call(bf16[128,768]{1,0:T(8,128)(2,1)} %bitcast.38, bf16[128,256]{1,0:T(8,128)(2,1)} %bitcast.39), custom_call_target="tpu_custom_call" | custom-call | bytes 3145728 | tf_op jit(solution)/shard_map/gather_dp/pallas_call | solution.py:178
  48.3 0.0 all-gather.2.cloned.1.call-update
  48.4 0.0 copy-done.4
  48.4 0.3 compare_reduce_fusion
  48.6 0.1 constant_dynamic-slice_fusion
  48.7 0.1 and_reduce_fusion
  48.8 0.2 multiply_reduce_fusion
  49.0 0.2 select_reduce_fusion
  49.2 0.1 compare_convert_fusion
  49.2 0.2 broadcast_in_dim.38.qid_ref
  49.4 0.2 reshape.75.live_ref
  49.6 0.0 copy-done.1
  49.6 3.8 %fusion.refs_0_.q_ref = bf16[768,768]{1,0:T(8,128)(2,1)} fusion(bf16[768,1024]{1,0:T(8,128)(2,1)S(1)} %copy-done.1, bf16[1024,768]{1,0:T(8,128)(2,1)} %bitcast.40), kind=kOutput, calls=%fused_computation.1 | convolution fusion | flops 1208549376 | bytes 4325376 | tf_op jit(solution)/shard_map/dot_general | solution.py:439
  53.4 91.5 %gather_dp.3 = (bf16[8,768,512]{2,1,0:T(8,128)(2,1)}, bf16[4,1024,256]{2,1,0:T(8,128)(2,1)}) custom-call(bf16[768,768]{1,0:T(8,128)(2,1)} %fusion.refs_0_.q_ref, bf16[1024,256]{1,0:T(8,128)(2,1)} %bitcast.35), custom_call_target="tpu_custom_call" | custom-call | bytes 18874368 | tf_op jit(solution)/shard_map/gather_dp/pallas_call | solution.py:178
  144.9 0.1 convert_reduce_fusion.count_ref
  145.0 0.0 copy-start.3
  145.0 1.3 copy-done.3
  146.3 0.0 copy-start.5
  146.3 2.8 %copy-done.5 = bf16[8,768,512]{2,1,0:T(8,128)(2,1)S(1)} copy-done((bf16[8,768,512]{2,1,0:T(8,128)(2,1)S(1)}, bf16[8,768,512]{2,1,0:T(8,128)(2,1)}, u32[]{:S(2)}) %copy-start.5) | copy-done | bytes 6291480
  149.1 0.0 copy-start
  149.1 18.9 %attend.1.attn_ref = bf16[768,256]{1,0:T(8,128)(2,1)S(1)} custom-call(s32[6,52]{1,0:T(8,128)S(1)} %pad.4.pages_ref, s32[6]{0:T(128)S(1)} %convert_reduce_fusion.count_ref, bf16[768,768]{1,0:T(8,128)(2,1)S(1)} %copy-done.3, bf16[6144,512]{1,0:T(8,128)(2,1)S(1)} %bitcast.30, s32[768,1]{1,0:T(8,128)S(1)} %broadcast_in_dim.38.qid_ref, s32[48,128]{1,0:T(8,128)S(1)} %copy-done.4), custom_call_target="tpu_custom_call" | custom-call | flops 9663676416 | bytes 6291456 | tf_op jit(solution)/shard_map/attend/pallas_call | solution.py:275
  168.0 0.0 all-gather.2.cloned.1.call-done.ffw_ref
  168.1 0.0 copy-done
  168.1 0.0 copy-start.2
  168.1 1.4 copy-done.2
  169.5 54.8 %tail.1 = bf16[768,1024]{1,0:T(8,128)(2,1)S(1)} custom-call(bf16[768,256]{1,0:T(8,128)(2,1)S(1)} %attend.1.attn_ref, bf16[768,1024]{1,0:T(8,128)(2,1)S(1)} %copy-done.2, bf16[1024,2048]{1,0:T(8,128)(2,1)} %all-gather.2.cloned.1.call-done.ffw_ref, bf16[4,1024,256]{2,1,0:T(8,128)(2,1)S(1)} %copy-done, f32[768,1]{1,0:T(8,128)S(1)} %reshape.75.live_ref), custom_call_target="tpu_custom_call" | custom-call | tf_op jit(solution)/shard_map/tail/pallas_call | solution.py:394
  224.3 1.1 copy.32
  (7 shorter events, 0.1 us)
Async XLA Ops:
  6.5 2.2 copy-start.6
  6.5 161.5 %all-gather.2.cloned.1.call-start = ((), (), s32[]{:S(2)}) async-start(), calls=%async_computation | async-start | bytes 4718592 | tf_op jit(solution)/shard_map/all_gather | solution.py:438
  8.7 1.6 copy-start.7
  11.0 37.3 %copy-start.4 = (s32[48,128]{1,0:T(8,128)S(1)}, s32[48,128]{1,0:T(8,128)}, u32[]{:S(2)}) copy-start(s32[48,128]{1,0:T(8,128)} %kid_ref.1) | copy-start | bytes 73732
  11.0 38.5 %copy-start.1 = (bf16[768,1024]{1,0:T(8,128)(2,1)S(1)}, bf16[768,1024]{1,0:T(8,128)(2,1)}, u32[]{:S(2)}) copy-start(bf16[768,1024]{1,0:T(8,128)(2,1)} %tok_ref.1) | copy-start | bytes 4718596
  145.0 1.3 copy-start.3
  146.3 2.8 %copy-start.5 = (bf16[8,768,512]{2,1,0:T(8,128)(2,1)S(1)}, bf16[8,768,512]{2,1,0:T(8,128)(2,1)}, u32[]{:S(2)}) copy-start(bf16[8,768,512]{2,1,0:T(8,128)(2,1)} %get-tuple-element.20) | copy-start | bytes 18874372
  149.1 19.0 %copy-start = (bf16[4,1024,256]{2,1,0:T(8,128)(2,1)S(1)}, bf16[4,1024,256]{2,1,0:T(8,128)(2,1)}, u32[]{:S(2)}) copy-start(bf16[4,1024,256]{2,1,0:T(8,128)(2,1)} %get-tuple-element.22.wout_ref) | copy-start | bytes 6291460
  168.1 1.4 copy-start.2
Sparse Core Ops, SparseCore 0:
  48.5 61.9 all-gather.1

commit v3 on v2

--- a/solution.py
+++ b/solution.py
@@ -29,51 +29,78 @@
     pl.semaphore_wait(barrier, count)
 
 
-def exchange_kernel(groups, count, *refs):
-    x_refs, out_refs = refs[:count], refs[count : 2 * count]
-    send_sem, recv_sem, local_sem = refs[2 * count :]
-    dp = lax.axis_index("dp")
-    me = lax.axis_index("tensor")
-    greet([(None, (dp, lax.rem(me + k, groups))) for k in range(1, groups)])
-    sends = []
-    for n in range(count):
-        for k in range(1, groups):
-            peer = lax.rem(me + k, groups)
-            copy = pltpu.make_async_remote_copy(
-                x_refs[n].at[peer], out_refs[n].at[me], send_sem.at[n, k], recv_sem.at[n, k],
-                device_id=(dp, peer), device_id_type=MESH,
-            )
-            copy.start()
-            sends.append(copy)
-        local = pltpu.make_async_copy(x_refs[n].at[me], out_refs[n].at[me], local_sem.at[n])
-        local.start()
-        sends.append(local)
-    for copy in sends:
-        copy.wait()
-
-
-def exchange(arrays, groups, cid):
-    count = len(arrays)
-    hbm = pl.BlockSpec(memory_space=pl.ANY)
-    return pl.pallas_call(
-        functools.partial(exchange_kernel, groups, count),
-        out_shape=[jax.ShapeDtypeStruct(x.shape, x.dtype) for x in arrays],
-        in_specs=[hbm] * count,
-        out_specs=[hbm] * count,
-        scratch_shapes=[
-            pltpu.SemaphoreType.DMA((count, groups)),
-            pltpu.SemaphoreType.DMA((count, groups)),
-            pltpu.SemaphoreType.DMA((count,)),
-        ],
-        compiler_params=pltpu.CompilerParams(collective_id=cid, has_side_effects=True),
-        name="exchange",
-    )(*arrays)
-
-
 def gather_kernel(chips, count, cols, groups, *refs):
     total = count + (1 if groups else 0)
     x_refs, out_refs = list(refs[:total]), refs[total : 2 * total]
-    right_sem, left_sem, core_sem, recv_sem, local_sem, side_send, side_recv = refs[2 * total :]
+    gather_body(chips, count, cols, groups, x_refs, out_refs, refs[2 * total :], True)
+
+
+def front_kernel(chips, groups, count, every, *refs):
+    x_refs, full_refs = refs[:every], refs[every : every + count]
+    late_refs, refs = refs[every + count : 2 * every], refs[2 * every :]
+    held, send_sem, recv_sem, own_sem = refs[:count], refs[count], refs[count + 1], refs[count + 2]
+    dp = lax.axis_index("dp")
+    me = lax.axis_index("tensor")
+    landing = list(held) + list(late_refs)
+
+    def swap(n, k):
+        peer = lax.rem(me + k, groups)
+        return pltpu.make_async_remote_copy(
+            x_refs[n].at[peer], landing[n].at[me], send_sem.at[n, k], recv_sem.at[n, k],
+            device_id=(dp, peer), device_id_type=MESH,
+        )
+
+    def keep(n):
+        return pltpu.make_async_copy(x_refs[n].at[me], landing[n].at[me], own_sem.at[n])
+
+    def begin():
+        for n in range(every):
+            for k in range(1, groups):
+                swap(n, k).start()
+            keep(n).start()
+        for n in range(count):
+            for k in range(1, groups):
+                swap(n, k).wait()
+            keep(n).wait()
+
+    gather_body(chips, count, None, groups, held, full_refs, refs[count + 3 :], False, begin)
+    for n in range(count, every):
+        for k in range(1, groups):
+            swap(n, k).wait()
+        keep(n).wait()
+
+
+def front(arrays, count, groups, cid):
+    dps = lax.axis_size("dp")
+    chips = dps // 2
+    every = len(arrays)
+    hbm = pl.BlockSpec(memory_space=pl.ANY)
+    return pl.pallas_call(
+        functools.partial(front_kernel, chips, groups, count, every),
+        out_shape=[jax.ShapeDtypeStruct((dps,) + x.shape, BF) for x in arrays[:count]]
+        + [jax.ShapeDtypeStruct(x.shape, BF) for x in arrays[count:]],
+        in_specs=[hbm] * every,
+        out_specs=[hbm] * every,
+        scratch_shapes=[pltpu.VMEM(x.shape, BF) for x in arrays[:count]]
+        + [
+            pltpu.SemaphoreType.DMA((every, groups)),
+            pltpu.SemaphoreType.DMA((every, groups)),
+            pltpu.SemaphoreType.DMA((every,)),
+            pltpu.SemaphoreType.DMA((count, chips)),
+            pltpu.SemaphoreType.DMA((count, chips)),
+            pltpu.SemaphoreType.DMA((count, chips)),
+            pltpu.SemaphoreType.DMA((count, dps)),
+            pltpu.SemaphoreType.DMA((count + 1,)),
+            pltpu.SemaphoreType.DMA((groups,)),
+            pltpu.SemaphoreType.DMA((groups,)),
+        ],
+        compiler_params=pltpu.CompilerParams(collective_id=cid, has_side_effects=True),
+        name="front",
+    )(*arrays)
+
+
+def gather_body(chips, count, cols, groups, x_refs, out_refs, sems, with_side, begin=None):
+    right_sem, left_sem, core_sem, recv_sem, local_sem, side_send, side_recv = sems
     dp = lax.axis_index("dp")
     tensor = lax.axis_index("tensor")
     chip, core = dp // 2, lax.rem(dp, 2)
@@ -89,6 +116,8 @@
     )
     if cols is not None:
         x_refs[0] = x_refs[0].at[:, cols[0] : cols[1]]
+    if begin is not None:
+        begin()
 
     def copy_of(n, source, block, send, device):
         return pltpu.make_async_remote_copy(
@@ -110,14 +139,14 @@
     for n in range(count):
         pltpu.make_async_copy(x_refs[n], out_refs[n].at[dp], local_sem.at[n]).start()
     side = []
-    for k, peer in enumerate(peers):
+    for k, peer in enumerate(peers if with_side else []):
         side.append(
             pltpu.make_async_remote_copy(
                 x_refs[count], out_refs[count].at[tensor], side_send.at[k], side_recv.at[k],
                 device_id=peer, device_id_type=MESH,
             )
         )
-    if groups:
+    if with_side:
         side.append(
             pltpu.make_async_copy(
                 x_refs[count], out_refs[count].at[tensor], local_sem.at[count]
@@ -304,7 +333,7 @@
 
 
 def tail_kernel(
-    groups, attn_ref, tok_ref, ffw_ref, wout_ref, live_ref, out_ref,
+    groups, attn_ref, tok_ref, up_ref, down_ref, wout_ref, live_ref, out_ref,
     heads_buf, wout, part_out, part_in, result,
     attn_send, attn_recv, part_send, part_recv, out_send, out_recv, local_sem,
 ):
@@ -312,7 +341,6 @@
     me = lax.axis_index("tensor")
     rows = attn_ref.shape[0] // groups
     width = attn_ref.shape[1]
-    ff = ffw_ref.shape[1] // 2
 
     def span(j):
         return pl.ds(pl.multiple_of(j * rows, rows), rows)
@@ -358,10 +386,10 @@
             attn, wout[...], (((1,), (1,)), ((), ())), preferred_element_type=F32
         )
         first = norm(tok_ref[at, :].astype(F32) + proj).astype(BF)
-        hidden = jnp.dot(first, ffw_ref[:, :ff], preferred_element_type=F32)
+        hidden = jnp.dot(first, up_ref[...], preferred_element_type=F32)
         inner = (0.5 * hidden * (1.0 + lax.erf(hidden * 0.7071067811865476))).astype(BF)
         part = lax.dot_general(
-            inner, ffw_ref[:, ff:], (((1,), (1,)), ((), ())), preferred_element_type=F32
+            inner, down_ref[...], (((1,), (1,)), ((), ())), preferred_element_type=F32
         )
         if i < groups - 1:
             part_out[i] = part.astype(BF)
@@ -386,7 +414,7 @@
     final.wait()
 
 
-def tail(attn, tokens, ffw, wout, live, groups, cid):
+def tail(attn, tokens, up, down, wout, live, groups, cid):
     rows, width = attn.shape
     wide = tokens.shape[1]
     share = rows // groups
@@ -394,7 +422,7 @@
     return pl.pallas_call(
         functools.partial(tail_kernel, groups),
         out_shape=jax.ShapeDtypeStruct(tokens.shape, BF),
-        in_specs=[vmem] * 5,
+        in_specs=[vmem] * 6,
         out_specs=pl.BlockSpec(memory_space=pl.ANY),
         scratch_shapes=[
             pltpu.VMEM((groups, rows, width), BF),
@@ -414,7 +442,7 @@
             collective_id=cid, has_side_effects=True, vmem_limit_bytes=48 * 2**20
         ),
         name="tail",
-    )(attn, tokens, ffw, wout, live)
+    )(attn, tokens, up, down, wout, live)
 
 
 def shards(tokens, w_qkv, w_out, w_up, w_down, slot_request):
@@ -429,24 +457,22 @@
     qkv_w = jnp.transpose(qkv_w, (1, 0, 3, 2, 4)).reshape(groups, slab, 3 * width)
     up_w = jnp.transpose(w_up.astype(BF).reshape(slab, groups, -1), (1, 0, 2))
     down_w = jnp.transpose(w_down.astype(BF).reshape(groups, -1, slab), (0, 2, 1))
-    ffw = jnp.concatenate([up_w, down_w], axis=2)
     out_w = jnp.transpose(w_out.astype(BF).reshape(groups, width, slab), (0, 2, 1))
-    mine = exchange([qkv_w, out_w, ffw], groups, 0)
-    mine = [x.reshape(groups * slab, x.shape[2]) for x in mine]
-    qkv_block, out_block = gather_dp(mine[:2], 1)
-    late, qkv_block = lax.optimization_barrier((mine[2], qkv_block))
-    ffw = lax.all_gather(late, "dp", axis=0, tiled=True)
+    qkv_block, out_block, up_part, down_part = front([qkv_w, out_w, up_w, down_w], 2, groups, 0)
+    up = lax.all_gather(up_part.reshape(groups * slab, -1), "dp", axis=0, tiled=True)
     qkv = jnp.dot(
         tokens, qkv_block.reshape(wide, 3 * width), preferred_element_type=F32
     ).astype(BF)
     kv, wout = gather_dp(
         [qkv], 2, cols=(width, 3 * width), side=out_block.reshape(wide, width), groups=groups
     )
+    down_part, up, kv = lax.optimization_barrier((down_part, up, kv))
+    down = lax.all_gather(down_part.reshape(groups * slab, -1), "dp", axis=0, tiled=True)
     kv = kv.reshape(-1, 2 * width)
     attn = attend(qkv, kv, slot_request, dp)
     own_ids = lax.dynamic_slice_in_dim(slot_request.reshape(-1), dp * rows, rows, 0)
     live = (own_ids >= 0).astype(F32)[:, None]
-    return tail(attn, tokens, ffw, wout, live, groups, 3)
+    return tail(attn, tokens, up, down, wout, live, groups, 3)
 
 
 def solution(mesh):

time: 235 us -> 218 us (0.928); the launches traced: 232 us -> 218 us
  Pallas kernels: 202 us -> 187 us
    pallas_call x2 -> x1, Pallas kernels: 114 us -> 75.6 us  [gather_dp(): pl.pallas_call(functools.partial(gather_kernel, chips, count, cols, group...]
    pallas_call x1, Pallas kernels: 13.8 us -> 29.1 us  [front(): pl.pallas_call(functools.partial(front_kernel, chips, groups, count, ever...]
    pallas_call x1, Pallas kernels: 54.8 us -> 59.9 us  [tail(): pl.pallas_call(functools.partial(tail_kernel, groups), out_shape=jax.Shap...]
    pallas_call x1, Pallas kernels: 18.9 us -> 22.4 us  [attend(): pl.pallas_call(functools.partial(attend_kernel, heads, page), out_shape=j...]
  transfers between devices with their start and end apart: 1 -> 2, of which waited for: 0 -> 0; matrix products, arithmetic and copies ran while one was open for 2% -> 2% of each run, Pallas kernels for 48% -> 45%
where the time goes in v3:
time: 218 us
  Pallas kernels  187 us (86%)
  between operations  13.6 us (6%)
  local copies, waits for them, and re-layouts  10.1 us (5%)
  matrix products  3.8 us (2%)
  other arithmetic  3.09 us (1%)
    pallas_call x1, Pallas kernels, gather_dp(): pl.pallas_call(functools.partial(gather_kernel, chips, count, cols, group...  75.6 us
    pallas_call x1, Pallas kernels, tail(): pl.pallas_call(functools.partial(tail_kernel, groups), out_shape=jax.Shap...  59.9 us
    pallas_call x1, Pallas kernels, front(): pl.pallas_call(functools.partial(front_kernel, chips, groups, count, ever...  29.1 us
    pallas_call x1, Pallas kernels, attend(): pl.pallas_call(functools.partial(attend_kernel, heads, page), out_shape=j...  22.4 us
    unnamed x17, local copies, waits for them, and re-layouts  6.69 us
  transfers between devices with their start and end apart: 2, of which 0 were waited for; matrix products, arithmetic and copies ran while one was open for 2% of the time, Pallas kernels for 45%

profile of v3, /device:TPU:0, one launch (start us, length us, event | category | flops | bytes accessed | tf_op | source)
XLA Modules:
  0.0 217.7 jit_solution(7862077434285852252)
XLA Ops:
  6.5 0.0 copy-start.6
  6.5 0.0 all-gather.3.cloned.1.call-start
  6.5 1.1 convert_element_type.36
  7.7 1.1 convert_element_type.37
  8.7 0.0 copy-done.6
  8.7 0.0 copy-start.7
  8.8 0.4 reshape.59
  9.2 0.2 copy.16
  9.4 0.0 copy-start.1
  9.4 0.9 reshape.60.refs_0_
  10.4 0.0 copy-done.7
  10.4 0.6 copy.30
  11.0 0.8 bitcast_bitcast_fusion
  11.8 29.1 %front.1 = (bf16[8,4,32,768]{3,2,1,0:T(8,128)(2,1)}, bf16[8,4,32,256]{3,2,1,0:T(8,128)(2,1)}, bf16[4,32,1024]{2,1,0:T(8,128)(2,1)}, bf16[4,32,1024]{2,1,0:T(8,128)(2,1)}) custom-call(bf16[4,32,768]{2,1,0:T(8,128)(2,1)} %reshape.60.refs_0_, bf16[4,32,256]{2,1,0:T(8,128)(2,1)} %bitcast.34, bf16[4,32,1024]{2,1,0:T(8,128)(2,1)} %get-tuple-element.26.refs_2_, ...), custom_call_target="tpu_custom_call" | custom-call | tf_op jit(solution)/shard_map/front/pallas_call | solution.py:78
  40.9 0.0 all-gather.3.cloned.1.call-update
  40.9 0.0 all-gather.5.cloned.1.call-start
  41.0 0.0 copy-done.1
  41.0 3.8 %fusion.refs_0_.q_ref = bf16[768,768]{1,0:T(8,128)(2,1)} fusion(bf16[768,1024]{1,0:T(8,128)(2,1)S(1)} %copy-done.1, bf16[1024,768]{1,0:T(8,128)(2,1)} %bitcast.38), kind=kOutput, calls=%fused_computation.1 | convolution fusion | flops 1208549376 | bytes 4325376 | tf_op jit(solution)/shard_map/dot_general | solution.py:463
  44.8 0.0 copy-start.4
  44.8 75.6 %gather_dp.1 = (bf16[8,768,512]{2,1,0:T(8,128)(2,1)}, bf16[4,1024,256]{2,1,0:T(8,128)(2,1)}) custom-call(bf16[768,768]{1,0:T(8,128)(2,1)} %fusion.refs_0_.q_ref, bf16[1024,256]{1,0:T(8,128)(2,1)} %bitcast.33), custom_call_target="tpu_custom_call" | custom-call | bytes 18874368 | tf_op jit(solution)/shard_map/gather_dp/pallas_call | solution.py:207
  120.4 0.0 all-gather.3.cloned.1.call-done.up_ref
  120.4 0.0 all-gather.5.cloned.1.call-update
  120.5 0.0 copy-done.4
  120.5 0.3 compare_reduce_fusion
  120.8 0.1 constant_dynamic-slice_fusion
  120.8 0.1 and_reduce_fusion
  120.9 0.2 multiply_reduce_fusion
  121.1 0.2 select_reduce_fusion
  121.3 0.1 compare_convert_fusion
  121.4 0.2 broadcast_in_dim.38.qid_ref
  121.5 0.2 reshape.71.live_ref
  121.7 0.1 convert_reduce_fusion.count_ref
  121.8 0.0 copy-start.3
  121.8 1.3 copy-done.3
  123.1 0.0 copy-start.5
  123.1 2.8 %copy-done.5 = bf16[8,768,512]{2,1,0:T(8,128)(2,1)S(1)} copy-done((bf16[8,768,512]{2,1,0:T(8,128)(2,1)S(1)}, bf16[8,768,512]{2,1,0:T(8,128)(2,1)}, u32[]{:S(2)}) %copy-start.5) | copy-done | bytes 6291480
  126.0 0.0 copy-start
  126.0 22.4 %attend.1.attn_ref = bf16[768,256]{1,0:T(8,128)(2,1)S(1)} custom-call(s32[6,52]{1,0:T(8,128)S(1)} %pad.4.pages_ref, s32[6]{0:T(128)S(1)} %convert_reduce_fusion.count_ref, bf16[768,768]{1,0:T(8,128)(2,1)S(1)} %copy-done.3, bf16[6144,512]{1,0:T(8,128)(2,1)S(1)} %bitcast.29, s32[768,1]{1,0:T(8,128)S(1)} %broadcast_in_dim.38.qid_ref, s32[48,128]{1,0:T(8,128)S(1)} %copy-done.4), custom_call_target="tpu_custom_call" | custom-call | flops 9663676416 | bytes 6291456 | tf_op jit(solution)/shard_map/attend/pallas_call | solution.py:304
  148.3 0.0 all-gather.5.cloned.1.call-done.down_ref
  148.4 0.0 copy-done
  148.4 0.0 copy-start.2
  148.4 1.4 copy-done.2
  149.8 59.9 %tail.1 = bf16[768,1024]{1,0:T(8,128)(2,1)S(1)} custom-call(bf16[768,256]{1,0:T(8,128)(2,1)S(1)} %attend.1.attn_ref, bf16[768,1024]{1,0:T(8,128)(2,1)S(1)} %copy-done.2, bf16[1024,1024]{1,0:T(8,128)(2,1)S(1)} %copy-done, bf16[1024,1024]{1,0:T(8,128)(2,1)} %all-gather.5.cloned.1.call-done.down_ref, bf16[4,1024,256]{2,1,0:T(8,128)(2,1)} %get-tuple-element.22.wout_ref, ...), custom_call_target="tpu_custom_call" | custom-call | tf_op jit(solution)/shard_map/tail/pallas_call | solution.py:422
  209.7 1.1 copy.32
  (6 shorter events, 0.1 us)
Async XLA Ops:
  6.5 2.2 %copy-start.6 = (f32[32,3072]{1,0:T(8,128)S(1)}, f32[32,3072]{1,0:T(8,128)}, u32[]{:S(2)}) copy-start(f32[32,3072]{1,0:T(8,128)} %param.7) | copy-start | bytes 1179652
  6.5 113.9 %all-gather.3.cloned.1.call-start = ((), (), s32[]{:S(2)}) async-start(), calls=%async_computation | async-start | bytes 2359296 | tf_op jit(solution)/shard_map/all_gather | solution.py:462
  8.7 1.6 copy-start.7
  9.4 31.6 %copy-start.1 = (bf16[768,1024]{1,0:T(8,128)(2,1)S(1)}, bf16[768,1024]{1,0:T(8,128)(2,1)}, u32[]{:S(2)}) copy-start(bf16[768,1024]{1,0:T(8,128)(2,1)} %tok_ref.1) | copy-start | bytes 4718596
  40.9 107.4 %all-gather.5.cloned.1.call-start = ((), (), s32[]{:S(2)}) async-start(), calls=%async_computation.1 | async-start | bytes 2359296 | tf_op jit(solution)/shard_map/all_gather | solution.py:470
  44.8 75.7 %copy-start.4 = (s32[48,128]{1,0:T(8,128)S(1)}, s32[48,128]{1,0:T(8,128)}, u32[]{:S(2)}) copy-start(s32[48,128]{1,0:T(8,128)} %kid_ref.1) | copy-start | bytes 73732
  121.8 1.3 copy-start.3
  123.1 2.8 %copy-start.5 = (bf16[8,768,512]{2,1,0:T(8,128)(2,1)S(1)}, bf16[8,768,512]{2,1,0:T(8,128)(2,1)}, u32[]{:S(2)}) copy-start(bf16[8,768,512]{2,1,0:T(8,128)(2,1)} %get-tuple-element.19) | copy-start | bytes 18874372
  126.0 22.4 %copy-start = (bf16[1024,1024]{1,0:T(8,128)(2,1)S(1)}, bf16[1024,1024]{1,0:T(8,128)(2,1)}, u32[]{:S(2)}) copy-start(bf16[1024,1024]{1,0:T(8,128)(2,1)} %all-gather.3.cloned.1.call-done.up_ref) | copy-start | bytes 6291460
  148.4 1.4 copy-start.2
Sparse Core Ops, SparseCore 0:
  41.1 40.0 all-gather.2
  120.6 27.4 all-gather.4
